TPU v7x, 32 devices: a whole 2x2x4 slice. The times are simulated.
32 devices in a mesh: layer: 2 (over x), rows: 16 (over z, y, core).
Axes of the slice: x: 2, y: 2, z: 4, core: 2. Of those that a mesh axis runs over, the one named last changes fastest.
Arguments:
- down_sources: bfloat16 [2, 32, 16384], P('layer', None, 'rows'), may hold values from -6 to 6
- up_sources: bfloat16 [2, 32, 16384], P('layer', None, 'rows'), may hold values from -6 to 6
- down_tiles: bfloat16 [2, 1024, 128, 128], P('layer', 'rows'), may hold values from -0.1875 to 0.1875
- up_tiles: bfloat16 [2, 1024, 128, 128], P('layer', 'rows'), may hold values from -0.1875 to 0.1875
- tile_rows: int32 [2, 1024], P('layer', 'rows'), may hold values from 0 to 127, as said below
- tile_cols: int32 [2, 1024], P('layer', 'rows'), may hold values from 0 to 127, as said below
- shot_order: int32 [32], replicated, may hold values from 0 to 31, each once
Outputs:
- traces: bfloat16 [2, 32, 16384], P('layer', None, 'rows')
Inputs may be any that keep to these rules, and one draw needn't show every extreme that they name: `tile_rows`: in every layer, tile t lies in the tile rows of index t // 64 of the rows axis: 8 * (t // 64) to 8 * (t // 64) + 7. `tile_cols`: every tile's column differs from its row by at most 8. `shot_order`: A permutation of the shots.
All inputs are finite; a program needn't handle non-finite values.
Results may differ from a plain program's by a relative error of at most 0.011.
Values may be sent and summed in bfloat16 or wider, within the bound.
No kernel may reach another device: no remote copies, remote signals or barrier semaphores. Data moves between devices by JAX's collectives and lax.ppermute only.
A program may use at most 64 MiB of HBM per device.

v0:
```python
import jax
import jax.numpy as jnp
from jax import lax
from jax.sharding import PartitionSpec as P

TILE = 128


def padded(value, sides, width):
    for axis, dim in sides:
        devices, length = (lax.axis_size(axis), value.shape[dim])
        up = [(i, (i + 1) % devices) for i in range(devices - 1)]
        down = [(j, i) for i, j in up]
        last = lax.slice_in_dim(value, length - width, length, axis=dim)
        initial = lax.slice_in_dim(value, 0, width, axis=dim)
        before = lax.ppermute(last, axis, up)
        after = lax.ppermute(initial, axis, down)
        value = jnp.concatenate([before, value, after], axis=dim)
    return value


def from_behind(block, axis, distance):
    devices = range(lax.axis_size(axis))
    route = [(i - distance, i) for i in devices if i - distance in devices]
    return lax.ppermute(block, axis, route)


def widen_rows(trace):
    return padded(trace, (("rows", 2),), trace.shape[2])


def step_down(trace):
    return from_behind(trace, "layer", 1)


def step_up(trace):
    return from_behind(trace, "layer", -1)


def incoming_down(trace):
    return widen_rows(step_down(trace))


def incoming_up(trace):
    return widen_rows(step_up(trace))


def apply_layer(tiles, local_rows, cols, whole, first, count_rows):
    columns = whole.shape[1]
    blocks = whole[0].reshape(columns, -1, TILE)
    picked = jnp.take(blocks, cols - first, axis=1)
    product = jnp.einsum("tij,stj->sti", tiles, picked, preferred_element_type=jnp.float32)
    onehot = (local_rows[:, None] == jnp.arange(count_rows, dtype=jnp.int32)[None, :]).astype(
        jnp.float32
    )
    summed = jnp.einsum("sti,tr->sri", product, onehot, precision=lax.Precision.HIGHEST)
    return summed.reshape(1, columns, count_rows * TILE)


def advance(source, term):
    return (source.astype(jnp.float32) + term).astype(jnp.bfloat16)


def shards(down_sources, up_sources, down_tiles, up_tiles, tile_rows, tile_cols, shot_order):
    forward = jnp.take(down_sources, shot_order, axis=1)
    backward = jnp.take(up_sources, shot_order, axis=1)
    count_rows = forward.shape[2] // TILE
    local_rows = tile_rows[0] - lax.axis_index("rows") * count_rows
    first = (lax.axis_index("rows") - 1) * count_rows
    cols = tile_cols[0]
    turns = lax.axis_size("layer") - 1
    down_trace = forward
    up_trace = backward
    for turn in range(turns):
        whole = incoming_down(down_trace)
        down_trace = advance(
            forward, apply_layer(down_tiles[0], local_rows, cols, whole, first, count_rows)
        )
    for turn in range(turns):
        whole = incoming_up(up_trace)
        up_trace = advance(
            backward, apply_layer(up_tiles[0], local_rows, cols, whole, first, count_rows)
        )
    return (down_trace.astype(jnp.float32) + up_trace.astype(jnp.float32)).astype(jnp.bfloat16)


def solution(mesh):
    return jax.shard_map(
        shards,
        mesh=mesh,
        in_specs=(
            P("layer", None, "rows"),
            P("layer", None, "rows"),
            P("layer", "rows", None, None),
            P("layer", "rows", None, None),
            P("layer", "rows"),
            P("layer", "rows"),
            P(),
        ),
        out_specs=P("layer", None, "rows"),
        check_vma=False,
    )
```

profile of v0, /device:TPU:13, one launch (start us, length us, event | category | flops | bytes accessed | tf_op | source)
XLA Modules:
  0.0 33.8 jit_solution(8356977620512853390)
XLA Ops:
  0.0 0.0 copy-start
  0.0 0.8 %compare_select_fusion.1 = s32[32]{0:T(128)S(1)} fusion(s32[32]{0:T(128)} %param.17), kind=kLoop, calls=%fused_computation.34 | loop fusion | flops 96 | bytes 256 | tf_op jit(solution)/shard_map/jit(_take)/jit(_where)/select_n | solution.py:65
  0.8 0.7 %compare_and_fusion.1 = pred[32]{0:T(512)(128)(4,1)S(1)} fusion(s32[32]{0:T(128)} %param.17), kind=kLoop, calls=%fused_computation.38 | loop fusion | flops 192 | bytes 160 | tf_op jit(solution)/shard_map/jit(_take)/and | solution.py:65
  1.5 1.5 %gather_fusion = bf16[32,1024]{1,0:T(8,128)(2,1)S(1)} fusion(bf16[32,1024]{1,0:T(8,128)(2,1)} %bitcast.45, s32[1024]{0:T(1024)S(1)} %pad_clamp_fusion.1), kind=kCustom, calls=%fused_computation.clone | custom fusion | bytes 131200 | tf_op jit(solution)/shard_map/jit(_take)/gather | solution.py:65
  3.0 1.5 %gather_fusion.2 = bf16[32,1024]{1,0:T(8,128)(2,1)S(1)} fusion(bf16[32,1024]{1,0:T(8,128)(2,1)} %bitcast.46, s32[1024]{0:T(1024)S(1)} %pad_clamp_fusion.1), kind=kCustom, calls=%fused_computation.2.clone | custom fusion | bytes 131200 | tf_op jit(solution)/shard_map/jit(_take)/gather | solution.py:66
  4.5 0.1 bitcast_select_fusion
  4.6 1.3 %collective-permute-start.3 = (bf16[1,32,1024]{2,1,0:T(8,128)(2,1)S(1)}, bf16[1,32,1024]{2,1,0:T(8,128)(2,1)S(1)}, u32[]{:S(2)}, u32[]{:S(2)}) collective-permute-start(bf16[1,32,1024]{2,1,0:T(8,128)(2,1)S(1)} %get-tuple-element.9), channel_id=1, source_target_pairs={{16,0},{17,1},{18,2},{19,3},{20,4},{21,5},{22,6},{23,7},{24,8},{25... | collective-permute-start | bytes 196616 | tf_op jit(solution)/shard_map/ppermute | solution.py:25
  5.9 4.0 %collective-permute-start = (bf16[1,32,1024]{2,1,0:T(8,128)(2,1)S(1)}, bf16[1,32,1024]{2,1,0:T(8,128)(2,1)S(1)}, u32[]{:S(2)}, u32[]{:S(2)}) collective-permute-start(bf16[1,32,1024]{2,1,0:T(8,128)(2,1)S(1)} %get-tuple-element.10), channel_id=1, source_target_pairs={{0,16},{1,17},{2,18},{3,19},{4,20},{5,21},{6,22},{7,23},{8,24},{9,... | collective-permute-start | bytes 196616 | tf_op jit(solution)/shard_map/ppermute | solution.py:25
  9.9 0.7 %compare_and_fusion = (pred[64]{0:T(512)(128)(4,1)S(1)}, s32[64]{0:T(128)S(1)}) fusion(s32[1,64]{1,0:T(1,128)} %param.16, s32[]{:T(128)S(6)} %mul.7), kind=kLoop, calls=%fused_computation.37 | loop fusion | flops 448 | bytes 580 | tf_op jit(solution)/shard_map/jit(_take)/and | solution.py:51
  10.6 0.7 %subtract_bitcast_fusion = s32[64]{0:T(128)S(1)} fusion(s32[1,64]{1,0:T(1,128)} %param.15, s32[]{:T(128)S(6)} %mul.6), kind=kLoop, calls=%fused_computation.39 | loop fusion | flops 64 | bytes 516 | tf_op jit(solution)/shard_map/sub | solution.py:68
  11.3 0.0 collective-permute-done.3
  11.3 4.3 %collective-permute-start.4 = (bf16[1,32,1024]{2,1,0:T(8,128)(2,1)S(1)}, bf16[1,32,1024]{2,1,0:T(8,128)(2,1)S(1)}, u32[]{:S(2)}, u32[]{:S(2)}) collective-permute-start(bf16[1,32,1024]{2,1,0:T(8,128)(2,1)S(1)} %collective-permute-done.3), channel_id=1, source_target_pairs={{0,1},{1,2},{2,3},{3,4},{4,5},{5,6},{6,7},{7,8},{8,9},{9,10},{10,1... | collective-permute-start | bytes 196616 | tf_op jit(solution)/shard_map/ppermute | solution.py:16
  15.5 1.9 %collective-permute-start.5 = (bf16[1,32,1024]{2,1,0:T(8,128)(2,1)S(1)}, bf16[1,32,1024]{2,1,0:T(8,128)(2,1)S(1)}, u32[]{:S(2)}, u32[]{:S(2)}) collective-permute-start(bf16[1,32,1024]{2,1,0:T(8,128)(2,1)S(1)} %collective-permute-done.3), channel_id=1, source_target_pairs={{1,0},{2,1},{3,2},{4,3},{5,4},{6,5},{7,6},{8,7},{9,8},{10,9},{11,1... | collective-permute-start | bytes 196616 | tf_op jit(solution)/shard_map/ppermute | solution.py:17
  17.5 0.0 collective-permute-done
  17.5 4.5 %collective-permute-start.1 = (bf16[1,32,1024]{2,1,0:T(8,128)(2,1)S(1)}, bf16[1,32,1024]{2,1,0:T(8,128)(2,1)S(1)}, u32[]{:S(2)}, u32[]{:S(2)}) collective-permute-start(bf16[1,32,1024]{2,1,0:T(8,128)(2,1)S(1)} %collective-permute-done), channel_id=1, source_target_pairs={{0,1},{1,2},{2,3},{3,4},{4,5},{5,6},{6,7},{7,8},{8,9},{9,10},{10,1... | collective-permute-start | bytes 196616 | tf_op jit(solution)/shard_map/ppermute | solution.py:16
  22.0 1.9 %collective-permute-start.2 = (bf16[1,32,1024]{2,1,0:T(8,128)(2,1)S(1)}, bf16[1,32,1024]{2,1,0:T(8,128)(2,1)S(1)}, u32[]{:S(2)}, u32[]{:S(2)}) collective-permute-start(bf16[1,32,1024]{2,1,0:T(8,128)(2,1)S(1)} %collective-permute-done), channel_id=1, source_target_pairs={{1,0},{2,1},{3,2},{4,3},{5,4},{6,5},{7,6},{8,7},{9,8},{10,9},{11,1... | collective-permute-start | bytes 196616 | tf_op jit(solution)/shard_map/ppermute | solution.py:17
  24.0 0.0 collective-permute-done.4
  24.0 0.0 collective-permute-done.5
  24.1 0.7 %gather_fusion.3 = bf16[64,32,128]{2,1,0:T(8,128)(2,1)S(1)} fusion(bf16[32,24,128]{2,0,1:T(8,128)(2,1)S(1)} %copy.9, s32[1024]{0:T(1024)S(1)} %pad_clamp_fusion), kind=kCustom, calls=%fused_computation.3.clone | custom fusion | bytes 1048832 | tf_op jit(solution)/shard_map/jit(_take)/gather | solution.py:51
  24.7 0.0 copy-done
  24.7 1.2 %fusion = f32[64,32,128]{2,1,0:T(8,128)S(1)} fusion(bf16[1,64,128,128]{3,2,1,0:T(8,128)(2,1)S(1)} %copy-done, bf16[64,32,128]{2,1,0:T(8,128)(2,1)S(1)} %gather_fusion.3, pred[64]{0:T(512)(128)(4,1)S(1)} %get-tuple-element.6), kind=kOutput, calls=%fused_computation.4 | convolution fusion | flops 67371008 | bytes 3670080 | tf_op jit(solution)/shard_map/tij,stj->sti/dot_general | solution.py:52
  26.0 1.1 %convolution_bitcast_fusion = f32[32,8,128]{2,1,0:T(8,128)S(1)} fusion(f32[64,32,128]{2,1,0:T(8,128)S(1)} %fusion, s32[64]{0:T(128)S(1)} %subtract_bitcast_fusion), kind=kOutput, calls=%fused_computation.8 | convolution fusion | flops 25166336 | bytes 1179904 | tf_op jit(solution)/shard_map/sti,tr->sri/dot_general | solution.py:56
  27.1 0.0 collective-permute-done.1
  27.1 1.4 %collective-permute-done.2 = bf16[1,32,1024]{2,1,0:T(8,128)(2,1)S(1)} collective-permute-done((bf16[1,32,1024]{2,1,0:T(8,128)(2,1)S(1)}, bf16[1,32,1024]{2,1,0:T(8,128)(2,1)S(1)}, u32[]{:S(2)}, u32[]{:S(2)}) %collective-permute-start.2) | collective-permute-done | bytes 65568 | tf_op jit(solution)/shard_map/ppermute | solution.py:17
  28.6 0.7 %gather_fusion.1 = bf16[64,32,128]{2,1,0:T(8,128)(2,1)S(1)} fusion(bf16[32,24,128]{2,0,1:T(8,128)(2,1)S(1)} %copy.8, s32[1024]{0:T(1024)S(1)} %pad_clamp_fusion), kind=kCustom, calls=%fused_computation.1.clone | custom fusion | bytes 1048832 | tf_op jit(solution)/shard_map/jit(_take)/gather | solution.py:51
  29.3 2.8 %fusion.2 = f32[64,32,128]{2,1,0:T(8,128)S(1)} fusion(bf16[1,64,128,128]{3,2,1,0:T(8,128)(2,1)} %param.13, bf16[64,32,128]{2,1,0:T(8,128)(2,1)S(1)} %gather_fusion.1, pred[64]{0:T(512)(128)(4,1)S(1)} %get-tuple-element.6), kind=kOutput, calls=%fused_computation.6 | convolution fusion | flops 67371008 | bytes 3670080 | tf_op jit(solution)/shard_map/tij,stj->sti/dot_general | solution.py:52
  32.1 1.1 %convolution_bitcast_fusion.1 = f32[32,8,128]{2,1,0:T(8,128)S(1)} fusion(f32[64,32,128]{2,1,0:T(8,128)S(1)} %fusion.2, s32[64]{0:T(128)S(1)} %subtract_bitcast_fusion), kind=kOutput, calls=%fused_computation.9 | convolution fusion | flops 25166336 | bytes 1179904 | tf_op jit(solution)/shard_map/sti,tr->sri/dot_general | solution.py:56
  33.2 0.7 %add_convert_fusion = bf16[1,32,1024]{2,1,0:T(8,128)(2,1)} fusion(f32[1,32,1024]{2,1,0:T(8,128)S(1)} %reshape.50, bf16[1,32,1024]{2,1,0:T(8,128)(2,1)S(1)} %get-tuple-element.10, f32[1,32,1024]{2,1,0:T(8,128)S(1)} %reshape.51, bf16[1,32,1024]{2,1,0:T(8,128)(2,1)S(1)} %get-tuple-element.9), kind=kLoop, calls=%fused_computation.24 | loop fusion | flops 327680 | bytes 458752 | tf_op jit(solution)/shard_map/convert_element_type | solution.py:84
  (10 shorter events, 0.2 us)
Async XLA Ops:
  0.0 24.7 %copy-start = (bf16[1,64,128,128]{3,2,1,0:T(8,128)(2,1)S(1)}, bf16[1,64,128,128]{3,2,1,0:T(8,128)(2,1)}, u32[]{:S(2)}) copy-start(bf16[1,64,128,128]{3,2,1,0:T(8,128)(2,1)} %param.14) | copy-start | bytes 6291460
  4.6 6.6 %collective-permute-start.3 = (bf16[1,32,1024]{2,1,0:T(8,128)(2,1)S(1)}, bf16[1,32,1024]{2,1,0:T(8,128)(2,1)S(1)}, u32[]{:S(2)}, u32[]{:S(2)}) collective-permute-start(bf16[1,32,1024]{2,1,0:T(8,128)(2,1)S(1)} %get-tuple-element.9), channel_id=1, source_target_pairs={{16,0},{17,1},{18,2},{19,3},{20,4},{21,5},{22,6},{23,7},{24,8},{25... | collective-permute-start | bytes 196616 | tf_op jit(solution)/shard_map/ppermute | solution.py:25
  5.9 11.5 %collective-permute-start = (bf16[1,32,1024]{2,1,0:T(8,128)(2,1)S(1)}, bf16[1,32,1024]{2,1,0:T(8,128)(2,1)S(1)}, u32[]{:S(2)}, u32[]{:S(2)}) collective-permute-start(bf16[1,32,1024]{2,1,0:T(8,128)(2,1)S(1)} %get-tuple-element.10), channel_id=1, source_target_pairs={{0,16},{1,17},{2,18},{3,19},{4,20},{5,21},{6,22},{7,23},{8,24},{9,... | collective-permute-start | bytes 196616 | tf_op jit(solution)/shard_map/ppermute | solution.py:25
  11.3 12.7 %collective-permute-start.4 = (bf16[1,32,1024]{2,1,0:T(8,128)(2,1)S(1)}, bf16[1,32,1024]{2,1,0:T(8,128)(2,1)S(1)}, u32[]{:S(2)}, u32[]{:S(2)}) collective-permute-start(bf16[1,32,1024]{2,1,0:T(8,128)(2,1)S(1)} %collective-permute-done.3), channel_id=1, source_target_pairs={{0,1},{1,2},{2,3},{3,4},{4,5},{5,6},{6,7},{7,8},{8,9},{9,10},{10,1... | collective-permute-start | bytes 196616 | tf_op jit(solution)/shard_map/ppermute | solution.py:16
  15.5 8.4 %collective-permute-start.5 = (bf16[1,32,1024]{2,1,0:T(8,128)(2,1)S(1)}, bf16[1,32,1024]{2,1,0:T(8,128)(2,1)S(1)}, u32[]{:S(2)}, u32[]{:S(2)}) collective-permute-start(bf16[1,32,1024]{2,1,0:T(8,128)(2,1)S(1)} %collective-permute-done.3), channel_id=1, source_target_pairs={{1,0},{2,1},{3,2},{4,3},{5,4},{6,5},{7,6},{8,7},{9,8},{10,9},{11,1... | collective-permute-start | bytes 196616 | tf_op jit(solution)/shard_map/ppermute | solution.py:17
  17.5 9.6 %collective-permute-start.1 = (bf16[1,32,1024]{2,1,0:T(8,128)(2,1)S(1)}, bf16[1,32,1024]{2,1,0:T(8,128)(2,1)S(1)}, u32[]{:S(2)}, u32[]{:S(2)}) collective-permute-start(bf16[1,32,1024]{2,1,0:T(8,128)(2,1)S(1)} %collective-permute-done), channel_id=1, source_target_pairs={{0,1},{1,2},{2,3},{3,4},{4,5},{5,6},{6,7},{7,8},{8,9},{9,10},{10,1... | collective-permute-start | bytes 196616 | tf_op jit(solution)/shard_map/ppermute | solution.py:16
  22.0 6.5 %collective-permute-start.2 = (bf16[1,32,1024]{2,1,0:T(8,128)(2,1)S(1)}, bf16[1,32,1024]{2,1,0:T(8,128)(2,1)S(1)}, u32[]{:S(2)}, u32[]{:S(2)}) collective-permute-start(bf16[1,32,1024]{2,1,0:T(8,128)(2,1)S(1)} %collective-permute-done), channel_id=1, source_target_pairs={{1,0},{2,1},{3,2},{4,3},{5,4},{6,5},{7,6},{8,7},{9,8},{10,9},{11,1... | collective-permute-start | bytes 196616 | tf_op jit(solution)/shard_map/ppermute | solution.py:17
where the time goes:
time: 34.2 us; the launch traced here: 33.8 us
  starting transfers between devices  17.9 us (52%)
  matrix products  6.16 us (18%)
  local copies, waits for them, and re-layouts  4.54 us (13%)
  other arithmetic  3.57 us (10%)
  waiting for transfers between devices  1.45 us (4%)
    ppermute x2, starting transfers between devices, padded(): before = lax.ppermute(last, axis, up)  8.8 us
    ppermute x2, starting transfers between devices, from_behind(): return lax.ppermute(block, axis, route)  5.28 us
    dot_general x2, matrix products, apply_layer(): jnp.einsum('tij,stj->sti', tiles, picked, preferred_element_type=jnp.floa...  4.05 us
    ppermute x2, starting transfers between devices, padded(): after = lax.ppermute(initial, axis, down)  3.84 us
    dot_general x2, matrix products, apply_layer(): jnp.einsum('sti,tr->sri', product, onehot, precision=lax.Precision.HIGHEST)  2.1 us
    gather x1, local copies, waits for them, and re-layouts, shards(): forward = jnp.take(down_sources, shot_order, axis=1)  1.52 us
    gather x1, local copies, waits for them, and re-layouts, shards(): backward = jnp.take(up_sources, shot_order, axis=1)  1.52 us
    ppermute x2, waiting for transfers between devices, padded(): after = lax.ppermute(initial, axis, down)  1.44 us
  transfers between devices with their start and end apart: 6, of which 1 were waited for; matrix products, arithmetic and copies ran while one was open for 13% of the time, Pallas kernels for 0%

commit v1 on v0

v1 whole, which is shorter than its diff:
```python
import functools

import jax
import jax.numpy as jnp
from jax import lax
from jax.experimental import pallas as pl
from jax.experimental.pallas import tpu as pltpu
from jax.sharding import PartitionSpec as P

TILE = 128
VMEM_BYTES = 32 * 1024 * 1024


def wavefront(layers):
    steps = []
    for t in range(layers - 1):
        down, up = (t, t + 1), (layers - 1 - t, layers - 2 - t)
        if down[0] == up[0] or down[1] == up[1]:
            steps += [(down, None), (None, up)]
        else:
            steps.append((down, up))
    return steps


def partner(r, rows):
    other = r ^ 1
    return other if other < rows else r


def farther(r, rows):
    other = r + 1 if r % 2 else r - 1
    return other if 0 <= other < rows else r


def exchange(block, moves, layers, rows):
    moves = [m for m in moves if m is not None]
    axes = ("layer", "rows")
    near = [(s * rows + r, d * rows + r) for s, d in moves for r in range(rows)]
    far = [(s * rows + r, d * rows + farther(r, rows)) for s, d in moves for r in range(rows)]
    inner = [(r, partner(r, rows)) for r in range(rows)]
    own = lax.ppermute(block, axes, near)
    distant = lax.ppermute(block, axes, far)
    beside = lax.ppermute(own, "rows", inner)
    return own, beside, distant


def pick_kernel(up_layer, down_tiles, up_tiles, picked, sem):
    upward = lax.axis_index("layer") == up_layer

    @pl.when(upward)
    def _():
        pltpu.make_async_copy(up_tiles.at[0], picked, sem).start()

    @pl.when(jnp.logical_not(upward))
    def _():
        pltpu.make_async_copy(down_tiles.at[0], picked, sem).start()

    pltpu.make_async_copy(down_tiles.at[0], picked, sem).wait()


def pick_tiles(down_tiles, up_tiles, up_layer):
    tiles = down_tiles.shape[1]
    size = down_tiles.size * down_tiles.dtype.itemsize
    return pl.pallas_call(
        functools.partial(pick_kernel, up_layer),
        out_shape=jax.ShapeDtypeStruct((tiles, TILE, TILE), down_tiles.dtype),
        in_specs=[pl.BlockSpec(memory_space=pltpu.HBM)] * 2,
        out_specs=pl.BlockSpec(memory_space=pltpu.VMEM),
        scratch_shapes=[pltpu.SemaphoreType.DMA],
        compiler_params=pltpu.CompilerParams(vmem_limit_bytes=VMEM_BYTES),
        cost_estimate=pl.CostEstimate(flops=0, bytes_accessed=2 * size, transcendentals=0),
        name="pick_tiles",
    )(down_tiles, up_tiles)


def apply_kernel(
    up_layer, down_layer, final,
    tile_rows, tile_cols, order, own, beside, distant, tiles, down, up, out, blocks, total,
):
    count = blocks.shape[0] // 3
    me = lax.axis_index("rows")
    layer = lax.axis_index("layer")
    for place, part in enumerate((own, beside, distant)):
        for k in range(count):
            blocks[place * count + k] = part[0, :, k * TILE:(k + 1) * TILE]
    total[...] = jnp.zeros_like(total)

    def one_tile(t, carry):
        row = tile_rows[0, t] - me * count
        col = tile_cols[0, t]
        index = col // count
        place = jnp.where(index == me, 0, jnp.where(index == (me ^ 1), 1, 2))
        seen = blocks[place * count + col - index * count]
        total[row] += lax.dot_general(
            tiles[t], seen, (((1,), (1,)), ((), ())), preferred_element_type=jnp.float32
        )
        return carry

    lax.fori_loop(0, tiles.shape[0], one_tile, 0, unroll=True)

    upward = layer == up_layer
    active = jnp.logical_or(upward, layer == down_layer)
    shots = own.shape[1]
    if final:
        slots = lax.broadcasted_iota(jnp.int32, (shots, shots), 0)
        onehot = (slots == order[...]).astype(jnp.float32).T.astype(jnp.bfloat16)
    for k in range(count):
        here = slice(k * TILE, (k + 1) * TILE)
        term = jnp.where(active, total[k].T, 0.0)
        below = down[0, :, here].astype(jnp.float32)
        above = up[0, :, here].astype(jnp.float32)
        base = jnp.where(upward, above, below)
        fresh = (base + term).astype(jnp.bfloat16)
        if final:
            rest = jnp.where(upward, below, above)
            both = (fresh.astype(jnp.float32) + rest).astype(jnp.bfloat16)
            fresh = jnp.dot(onehot, both, preferred_element_type=jnp.float32).astype(jnp.bfloat16)
        out[0, :, here] = fresh


def apply_step(tile_rows, tile_cols, order, parts, tiles, down, up, moves, final):
    _, shots, width = down.shape
    count = width // TILE
    down_move, up_move = moves
    vmem = pl.BlockSpec(memory_space=pltpu.VMEM)
    smem = pl.BlockSpec(memory_space=pltpu.SMEM)
    kernel = functools.partial(
        apply_kernel, up_move[1] if up_move else -1, down_move[1] if down_move else -1, final
    )
    return pl.pallas_call(
        kernel,
        out_shape=jax.ShapeDtypeStruct(down.shape, down.dtype),
        in_specs=[smem, smem] + [vmem] * 7,
        out_specs=vmem,
        scratch_shapes=[
            pltpu.VMEM((3 * count, shots, TILE), jnp.bfloat16),
            pltpu.VMEM((count, TILE, shots), jnp.float32),
        ],
        compiler_params=pltpu.CompilerParams(vmem_limit_bytes=VMEM_BYTES),
        cost_estimate=pl.CostEstimate(
            flops=2 * tiles.size * shots, bytes_accessed=tiles.size * 2, transcendentals=0
        ),
        name="apply_step",
    )(tile_rows, tile_cols, order, *parts, tiles, down, up)


def shards(down_sources, up_sources, down_tiles, up_tiles, tile_rows, tile_cols, shot_order):
    layers, rows = lax.axis_size("layer"), lax.axis_size("rows")
    layer = lax.axis_index("layer")
    order = shot_order.reshape(1, -1)
    steps = wavefront(layers)
    down, up = down_sources, up_sources
    for at, moves in enumerate(steps):
        down_move, up_move = moves
        final = at == len(steps) - 1
        if up_move is None:
            leaving = down
        elif down_move is None:
            leaving = up
        else:
            leaving = jnp.where(layer == up_move[0], up, down)
        parts = exchange(leaving, moves, layers, rows)
        tiles = pick_tiles(down_tiles, up_tiles, up_move[1] if up_move else -1)
        fresh = apply_step(tile_rows, tile_cols, order, parts, tiles, down, up, moves, final)
        if final:
            return fresh
        upward = layer == (up_move[1] if up_move else -1)
        down, up = jnp.where(upward, down, fresh), jnp.where(upward, fresh, up)


def solution(mesh):
    return jax.shard_map(
        shards,
        mesh=mesh,
        in_specs=(
            P("layer", None, "rows"),
            P("layer", None, "rows"),
            P("layer", "rows", None, None),
            P("layer", "rows", None, None),
            P("layer", "rows"),
            P("layer", "rows"),
            P(),
        ),
        out_specs=P("layer", None, "rows"),
        check_vma=False,
    )
```

time: 34.2 us -> 12.9 us (0.38)
  the two profiles are of different devices: /device:TPU:13 before, /device:TPU:31 now
where the time goes in v1:
time: 12.9 us; the launch traced here: 12.6 us
  starting transfers between devices  4.33 us (34%)
  local copies, waits for them, and re-layouts  3.2 us (25%)
  Pallas kernels  2.43 us (19%)
  waiting for transfers between devices  1.65 us (13%)
  other arithmetic  0.93 us (7%)
    unnamed x14, local copies, waits for them, and re-layouts  3.2 us
    ppermute x1, starting transfers between devices, exchange(): beside = lax.ppermute(own, 'rows', inner)  2.8 us
    pallas_call x1, Pallas kernels, apply_step(): pl.pallas_call(kernel, out_shape=jax.ShapeDtypeStruct(down.shape, down.dt...  2.28 us
    ppermute x1, waiting for transfers between devices, exchange(): own = lax.ppermute(block, axes, near)  1.65 us
    ppermute x1, starting transfers between devices, exchange(): distant = lax.ppermute(block, axes, far)  1.21 us
    select_n x1, other arithmetic, shards(): leaving = jnp.where(layer == up_move[0], up, down)  0.93 us
    ppermute x1, starting transfers between devices, exchange(): own = lax.ppermute(block, axes, near)  0.32 us
  transfers between devices with their start and end apart: 3, of which 1 were waited for; matrix products, arithmetic and copies ran while one was open for 0% of the time, Pallas kernels for 1%

profile of v1, /device:TPU:31, one launch (start us, length us, event | category | flops | bytes accessed | tf_op | source)
XLA Modules:
  0.0 12.6 jit_solution(9770599514693704864)
XLA Ops:
  0.0 0.0 copy-start.2
  0.0 0.0 copy-start.3
  0.0 0.0 copy-start.4
  0.0 0.0 copy-start.5
  0.0 0.0 copy-start.6
  0.0 0.9 %broadcast_select_fusion = bf16[1,32,1024]{2,1,0:T(8,128)(2,1)S(1)} fusion(bf16[1,32,1024]{2,1,0:T(8,128)(2,1)} %up.1, bf16[1,32,1024]{2,1,0:T(8,128)(2,1)} %down.1, pred[]{:T(512)S(6)} %eq.3), kind=kLoop, calls=%fused_computation | loop fusion | flops 32768 | bytes 196609 | tf_op jit(solution)/shard_map/jit(_where)/select_n | solution.py:161
  1.0 0.3 %collective-permute-start = (bf16[1,32,1024]{2,1,0:T(8,128)(2,1)S(1)}, bf16[1,32,1024]{2,1,0:T(8,128)(2,1)S(1)}, u32[]{:S(2)}, u32[]{:S(2)}) collective-permute-start(bf16[1,32,1024]{2,1,0:T(8,128)(2,1)S(1)} %broadcast_select_fusion), channel_id=1, source_target_pairs={{0,16},{1,17},{2,18},{3,19},{4,20},{5,21},{6,22},{7,23},{8,24},{9,... | collective-permute-start | bytes 196616 | tf_op jit(solution)/shard_map/ppermute | solution.py:41
  1.3 1.2 %collective-permute-start.2 = (bf16[1,32,1024]{2,1,0:T(8,128)(2,1)S(1)}, bf16[1,32,1024]{2,1,0:T(8,128)(2,1)S(1)}, u32[]{:S(2)}, u32[]{:S(2)}) collective-permute-start(bf16[1,32,1024]{2,1,0:T(8,128)(2,1)S(1)} %broadcast_select_fusion), channel_id=1, source_target_pairs={{0,16},{1,18},{2,17},{3,20},{4,19},{5,22},{6,21},{7,24},{8,23},{9,... | collective-permute-start | bytes 196616 | tf_op jit(solution)/shard_map/ppermute | solution.py:42
  2.5 1.6 %collective-permute-done.own = bf16[1,32,1024]{2,1,0:T(8,128)(2,1)S(1)} collective-permute-done((bf16[1,32,1024]{2,1,0:T(8,128)(2,1)S(1)}, bf16[1,32,1024]{2,1,0:T(8,128)(2,1)S(1)}, u32[]{:S(2)}, u32[]{:S(2)}) %collective-permute-start) | collective-permute-done | bytes 65568 | tf_op jit(solution)/shard_map/ppermute | solution.py:41
  4.1 2.8 %collective-permute-start.1 = (bf16[1,32,1024]{2,1,0:T(8,128)(2,1)S(1)}, bf16[1,32,1024]{2,1,0:T(8,128)(2,1)S(1)}, u32[]{:S(2)}, u32[]{:S(2)}) collective-permute-start(bf16[1,32,1024]{2,1,0:T(8,128)(2,1)S(1)} %collective-permute-done.own), channel_id=1, source_target_pairs={{0,1},{1,0},{2,3},{3,2},{4,5},{5,4},{6,7},{7,6},{8,9},{9,8},{10,11... | collective-permute-start | bytes 196616 | tf_op jit(solution)/shard_map/ppermute | solution.py:43
  6.9 0.0 copy-start
  6.9 1.6 %copy-done = bf16[1,64,128,128]{3,2,1,0:T(8,128)(2,1)S(1)} copy-done((bf16[1,64,128,128]{3,2,1,0:T(8,128)(2,1)S(1)}, bf16[1,64,128,128]{3,2,1,0:T(8,128)(2,1)}, u32[]{:S(2)}) %copy-start) | copy-done | bytes 2097176
  8.5 0.0 copy-start.1
  8.5 1.6 %copy-done.1 = bf16[1,64,128,128]{3,2,1,0:T(8,128)(2,1)S(1)} copy-done((bf16[1,64,128,128]{3,2,1,0:T(8,128)(2,1)S(1)}, bf16[1,64,128,128]{3,2,1,0:T(8,128)(2,1)}, u32[]{:S(2)}) %copy-start.1) | copy-done | bytes 2097176
  10.1 0.1 %pick_tiles.1.tiles = bf16[64,128,128]{2,1,0:T(8,128)(2,1)S(1)} custom-call(bf16[1,64,128,128]{3,2,1,0:T(8,128)(2,1)S(1)} %copy-done, bf16[1,64,128,128]{3,2,1,0:T(8,128)(2,1)S(1)} %copy-done.1), custom_call_target="tpu_custom_call" | custom-call | bytes 4194304 | tf_op jit(solution)/shard_map/pick_tiles/pallas_call | solution.py:64
  10.3 0.0 collective-permute-done.2.distant
  10.3 0.0 collective-permute-done.1.beside
  10.3 0.0 copy-done.2
  10.3 0.0 copy-done.3
  10.3 0.0 copy-done.4
  10.3 0.0 copy-done.5
  10.3 0.0 copy-done.6
  10.4 2.3 %apply_step.1 = bf16[1,32,1024]{2,1,0:T(8,128)(2,1)} custom-call(s32[1,64]{1,0:T(1,128)S(1)} %copy-done.4, s32[1,64]{1,0:T(1,128)S(1)} %copy-done.5, s32[1,32]{1,0:T(1,128)S(1)} %bitcast.1, bf16[1,32,1024]{2,1,0:T(8,128)(2,1)S(1)} %collective-permute-done.own, bf16[1,32,1024]{2,1,0:T(8,128)(2,1)S(1)} %collective-permute-done.1.beside, ...), custom_call_target="tpu_custom_call" | custom-call | flops 67108864 | bytes 2097152 | tf_op jit(solution)/shard_map/apply_step/pallas_call | solution.py:130
Async XLA Ops:
  0.0 10.3 %copy-start.2 = (bf16[1,32,1024]{2,1,0:T(8,128)(2,1)S(1)}, bf16[1,32,1024]{2,1,0:T(8,128)(2,1)}, u32[]{:S(2)}) copy-start(bf16[1,32,1024]{2,1,0:T(8,128)(2,1)} %up.1) | copy-start | bytes 196612
  0.0 10.3 %copy-start.3 = (bf16[1,32,1024]{2,1,0:T(8,128)(2,1)S(1)}, bf16[1,32,1024]{2,1,0:T(8,128)(2,1)}, u32[]{:S(2)}) copy-start(bf16[1,32,1024]{2,1,0:T(8,128)(2,1)} %down.1) | copy-start | bytes 196612
  0.0 10.3 %copy-start.4 = (s32[1,64]{1,0:T(1,128)S(1)}, s32[1,64]{1,0:T(1,128)}, u32[]{:S(2)}) copy-start(s32[1,64]{1,0:T(1,128)} %tile_rows.1) | copy-start | bytes 772
  0.0 10.3 %copy-start.5 = (s32[1,64]{1,0:T(1,128)S(1)}, s32[1,64]{1,0:T(1,128)}, u32[]{:S(2)}) copy-start(s32[1,64]{1,0:T(1,128)} %tile_cols.1) | copy-start | bytes 772
  0.0 10.3 %copy-start.6 = (s32[32]{0:T(128)S(1)}, s32[32]{0:T(128)}, u32[]{:S(2)}) copy-start(s32[32]{0:T(128)} %param.13) | copy-start | bytes 388
  1.0 3.2 %collective-permute-start = (bf16[1,32,1024]{2,1,0:T(8,128)(2,1)S(1)}, bf16[1,32,1024]{2,1,0:T(8,128)(2,1)S(1)}, u32[]{:S(2)}, u32[]{:S(2)}) collective-permute-start(bf16[1,32,1024]{2,1,0:T(8,128)(2,1)S(1)} %broadcast_select_fusion), channel_id=1, source_target_pairs={{0,16},{1,17},{2,18},{3,19},{4,20},{5,21},{6,22},{7,23},{8,24},{9,... | collective-permute-start | bytes 196616 | tf_op jit(solution)/shard_map/ppermute | solution.py:41
  1.3 9.0 %collective-permute-start.2 = (bf16[1,32,1024]{2,1,0:T(8,128)(2,1)S(1)}, bf16[1,32,1024]{2,1,0:T(8,128)(2,1)S(1)}, u32[]{:S(2)}, u32[]{:S(2)}) collective-permute-start(bf16[1,32,1024]{2,1,0:T(8,128)(2,1)S(1)} %broadcast_select_fusion), channel_id=1, source_target_pairs={{0,16},{1,18},{2,17},{3,20},{4,19},{5,22},{6,21},{7,24},{8,23},{9,... | collective-permute-start | bytes 196616 | tf_op jit(solution)/shard_map/ppermute | solution.py:42
  4.1 6.2 %collective-permute-start.1 = (bf16[1,32,1024]{2,1,0:T(8,128)(2,1)S(1)}, bf16[1,32,1024]{2,1,0:T(8,128)(2,1)S(1)}, u32[]{:S(2)}, u32[]{:S(2)}) collective-permute-start(bf16[1,32,1024]{2,1,0:T(8,128)(2,1)S(1)} %collective-permute-done.own), channel_id=1, source_target_pairs={{0,1},{1,0},{2,3},{3,2},{4,5},{5,4},{6,7},{7,6},{8,9},{9,8},{10,11... | collective-permute-start | bytes 196616 | tf_op jit(solution)/shard_map/ppermute | solution.py:43
  6.9 1.6 %copy-start = (bf16[1,64,128,128]{3,2,1,0:T(8,128)(2,1)S(1)}, bf16[1,64,128,128]{3,2,1,0:T(8,128)(2,1)}, u32[]{:S(2)}) copy-start(bf16[1,64,128,128]{3,2,1,0:T(8,128)(2,1)} %down_tiles.1) | copy-start | bytes 6291460
  8.5 1.6 %copy-start.1 = (bf16[1,64,128,128]{3,2,1,0:T(8,128)(2,1)S(1)}, bf16[1,64,128,128]{3,2,1,0:T(8,128)(2,1)}, u32[]{:S(2)}) copy-start(bf16[1,64,128,128]{3,2,1,0:T(8,128)(2,1)} %up_tiles.1) | copy-start | bytes 6291460

commit v2 on v1

v2 whole, which is shorter than its diff:
```python
import functools

import jax
import jax.numpy as jnp
from jax import lax
from jax.experimental import pallas as pl
from jax.experimental.pallas import tpu as pltpu
from jax.sharding import PartitionSpec as P

TILE = 128
VMEM_BYTES = 32 * 1024 * 1024


def wavefront(layers):
    steps = []
    for t in range(layers - 1):
        down, up = (t, t + 1), (layers - 1 - t, layers - 2 - t)
        if down[0] == up[0] or down[1] == up[1]:
            steps += [(down, None), (None, up)]
        else:
            steps.append((down, up))
    return steps


def partner(r, rows):
    other = r ^ 1
    return other if other < rows else r


def farther(r, rows):
    other = r + 1 if r % 2 else r - 1
    return other if 0 <= other < rows else r


def exchange(block, moves, layers, rows):
    moves = [m for m in moves if m is not None]
    axes = ("layer", "rows")
    near = [(s * rows + r, d * rows + r) for s, d in moves for r in range(rows)]
    far = [(s * rows + r, d * rows + farther(r, rows)) for s, d in moves for r in range(rows)]
    return lax.ppermute(block, axes, near), lax.ppermute(block, axes, far)


def beside_pairs(rows):
    return [(r, partner(r, rows)) for r in range(rows)]


def prepare_kernel(
    moves, final, down_tiles, up_tiles, tile_rows, tile_cols, order, down, up,
    tiles, lists, shuffle, base, rest, rows_here, cols_here, order_here, down_here, up_here, sems,
):
    count, shots = base.shape[0], base.shape[1]
    layer, me = lax.axis_index("layer"), lax.axis_index("rows")
    down_move, up_move = moves
    upward = layer == up_move[1] if up_move else layer < 0
    active = jnp.logical_or(upward, layer == down_move[1]) if down_move else upward

    small = [
        pltpu.make_async_copy(source, here, sems.at[1 + k])
        for k, (source, here) in enumerate((
            (tile_rows, rows_here), (tile_cols, cols_here), (order, order_here), (down, down_here), (up, up_here)
        ))
    ]
    for copy in small:
        copy.start()

    @pl.when(upward)
    def _():
        pltpu.make_async_copy(up_tiles.at[0], tiles, sems.at[0]).start()

    @pl.when(jnp.logical_not(upward))
    def _():
        pltpu.make_async_copy(down_tiles.at[0], tiles, sems.at[0]).start()

    for copy in small:
        copy.wait()

    n = tile_rows.shape[1]
    pairs = lists.shape[1]
    shift = (3 * count).bit_length()
    even = me % 2 == 0
    row = rows_here[...] - me * count
    seen = cols_here[...] - (me - 1) * count
    before = seen + jnp.where(even, 2 * count, count)
    after = seen - 2 * count + jnp.where(even, count, 2 * count)
    block = jnp.where(seen < count, before, jnp.where(seen < 2 * count, seen - count, after))
    block = jnp.where(active, block, 3 * count)

    def both_ways(value):
        across = jnp.broadcast_to(value.astype(jnp.float32), (n, n))
        return across, across.T

    row_l, row_s = both_ways(row)
    block_s = both_ways(block)[1][:, :1]
    t_l = lax.broadcasted_iota(jnp.int32, (n, n), 1)
    t_s = lax.broadcasted_iota(jnp.int32, (n, n), 0)
    same = row_l == row_s
    rank_l = jnp.sum(jnp.where(same & (t_s < t_l), 1.0, 0.0), axis=0, keepdims=True)
    rank_s = jnp.sum(jnp.where(same & (t_l < t_s), 1.0, 0.0), axis=1, keepdims=True)
    half_l, half_s = jnp.floor(rank_l * 0.5), jnp.floor(rank_s * 0.5)
    first_l, first_s = rank_l == 2.0 * half_l, rank_s == 2.0 * half_s
    ahead = jnp.sum(jnp.where((row_l < row_s) & first_l, 1.0, 0.0), axis=1, keepdims=True)
    place = ahead + half_s
    hit = place == lax.broadcasted_iota(jnp.int32, (n, pairs), 1).astype(jnp.float32)
    hit_a, hit_b = hit & first_s, hit & jnp.logical_not(first_s)

    def listed(hits, value):
        return jnp.sum(jnp.where(hits, value, 0.0), axis=0, keepdims=True)

    number = t_s[:, :1].astype(jnp.float32)
    nothing = 3.0 * count
    block_a = listed(hit_a, block_s - nothing) + nothing
    block_b = listed(hit_b, block_s - nothing) + nothing
    word = (listed(hit_a, row_s[:, :1]) * 2**shift + block_a) * 2**shift + block_b
    lists[0:1, :] = listed(hit_a, number).astype(jnp.int32)
    lists[1:2, :] = listed(hit_b, number).astype(jnp.int32)
    lists[2:3, :] = word.astype(jnp.int32)

    slots = lax.broadcasted_iota(jnp.int32, (shots, shots), 0)
    wanted = order_here[...] if final else lax.broadcasted_iota(jnp.int32, (shots, shots), 1)
    shuffle[...] = (slots == wanted).astype(jnp.float32).T.astype(jnp.bfloat16)
    for k in range(count):
        here = slice(k * TILE, (k + 1) * TILE)
        below, above = down_here[0, :, here], up_here[0, :, here]
        base[k] = jnp.where(upward, above, below).astype(jnp.float32)
        rest[k] = jnp.where(upward, below, above)
    pltpu.make_async_copy(down_tiles.at[0], tiles, sems.at[0]).wait()


def prepare(moves, final, down_tiles, up_tiles, tile_rows, tile_cols, order, down, up):
    tiles = down_tiles.shape[1]
    _, shots, width = down.shape
    count = width // TILE
    pairs = (tiles + min(tiles, count)) // 2
    vmem = pl.BlockSpec(memory_space=pltpu.VMEM)
    size = down_tiles.size * down_tiles.dtype.itemsize
    return pl.pallas_call(
        functools.partial(prepare_kernel, moves, final),
        out_shape=(
            jax.ShapeDtypeStruct((tiles, TILE, TILE), down_tiles.dtype),
            jax.ShapeDtypeStruct((3, pairs), jnp.int32),
            jax.ShapeDtypeStruct((shots, shots), jnp.bfloat16),
            jax.ShapeDtypeStruct((count, shots, TILE), jnp.float32),
            jax.ShapeDtypeStruct((count, shots, TILE), jnp.bfloat16),
        ),
        in_specs=[pl.BlockSpec(memory_space=pl.ANY)] * 7,
        out_specs=(vmem,) * 5,
        scratch_shapes=[
            pltpu.VMEM(value.shape, value.dtype) for value in (tile_rows, tile_cols, order, down, up)
        ] + [pltpu.SemaphoreType.DMA((6,))],
        compiler_params=pltpu.CompilerParams(vmem_limit_bytes=VMEM_BYTES),
        cost_estimate=pl.CostEstimate(flops=0, bytes_accessed=2 * size, transcendentals=0),
        name="prepare",
    )(*(
        pltpu.with_memory_space_constraint(value, pltpu.HBM)
        for value in (down_tiles, up_tiles, tile_rows, tile_cols, order, down, up)
    ))


def arrange_kernel(lists, tiles, weights):
    rows = lax.broadcasted_iota(jnp.int32, (TILE, TILE), 0)
    identity = (rows == lax.broadcasted_iota(jnp.int32, (TILE, TILE), 1)).astype(jnp.bfloat16)
    for p in range(weights.shape[0]):
        weights[p, :TILE] = tiles[lists[0, p]].T
        weights[p, TILE:] = lax.dot_general(
            identity, tiles[lists[1, p]], (((1,), (1,)), ((), ())), preferred_element_type=jnp.float32
        ).astype(jnp.bfloat16)


def arrange(lists, tiles):
    vmem = pl.BlockSpec(memory_space=pltpu.VMEM)
    pairs = lists.shape[1]
    return pl.pallas_call(
        arrange_kernel,
        out_shape=jax.ShapeDtypeStruct((pairs, 2 * TILE, TILE), tiles.dtype),
        in_specs=[vmem] * 2,
        out_specs=vmem,
        compiler_params=pltpu.CompilerParams(vmem_limit_bytes=VMEM_BYTES),
        cost_estimate=pl.CostEstimate(flops=0, bytes_accessed=2 * tiles.size * 2, transcendentals=0),
        name="arrange",
    )(lists, tiles)


def apply_kernel(lists, shuffle, own, beside, distant, weights, base, rest, out, blocks, total):
    count, shots = base.shape[0], base.shape[1]
    shift = (3 * count).bit_length()
    for place, part in enumerate((own, beside, distant)):
        for k in range(count):
            blocks[place * count + k] = part[0, :, k * TILE:(k + 1) * TILE]
    blocks[3 * count] = jnp.zeros((shots, TILE), jnp.bfloat16)
    total[...] = base[...]
    mask = 2**shift - 1
    for p in range(weights.shape[0]):
        word = lists[2, p]
        read = jnp.concatenate([blocks[(word >> shift) & mask], blocks[word & mask]], axis=1)
        total[word >> (2 * shift)] += jnp.dot(read, weights[p], preferred_element_type=jnp.float32)
    for k in range(count):
        fresh = total[k].astype(jnp.bfloat16)
        if rest is not None:
            fresh = (fresh.astype(jnp.float32) + rest[k].astype(jnp.float32)).astype(jnp.bfloat16)
        fresh = jnp.dot(shuffle[...], fresh, preferred_element_type=jnp.float32)
        out[0, :, k * TILE:(k + 1) * TILE] = fresh.astype(jnp.bfloat16)


def apply_step(lists, shuffle, parts, weights, base, rest, final):
    count, shots, _ = base.shape
    vmem = pl.BlockSpec(memory_space=pltpu.VMEM)

    def kernel(lists, shuffle, own, beside, distant, weights, base, rest, *others):
        apply_kernel(
            lists, shuffle, own, beside, distant, weights, base, rest if final else None, *others
        )

    return pl.pallas_call(
        kernel,
        out_shape=jax.ShapeDtypeStruct((1, shots, count * TILE), jnp.bfloat16),
        in_specs=[vmem] * 8,
        out_specs=vmem,
        scratch_shapes=[
            pltpu.VMEM((3 * count + 1, shots, TILE), jnp.bfloat16),
            pltpu.VMEM((count, shots, TILE), jnp.float32),
        ],
        compiler_params=pltpu.CompilerParams(vmem_limit_bytes=VMEM_BYTES),
        cost_estimate=pl.CostEstimate(
            flops=2 * weights.size * shots, bytes_accessed=weights.size * 2, transcendentals=0
        ),
        name="apply_step",
    )(lists, shuffle, *parts, weights, base, rest)


def shards(down_sources, up_sources, down_tiles, up_tiles, tile_rows, tile_cols, shot_order):
    layers, rows = lax.axis_size("layer"), lax.axis_size("rows")
    layer = lax.axis_index("layer")
    order = shot_order.reshape(1, -1)
    steps = wavefront(layers)
    down, up = down_sources, up_sources
    for at, moves in enumerate(steps):
        down_move, up_move = moves
        final = at == len(steps) - 1
        if up_move is None:
            leaving = down
        elif down_move is None:
            leaving = up
        else:
            leaving = jnp.where(layer == up_move[0], up, down)
        own, distant = exchange(leaving, moves, layers, rows)
        tiles, lists, shuffle, base, rest = prepare(
            moves, final, down_tiles, up_tiles, tile_rows, tile_cols, order, down, up
        )
        own, lists = lax.optimization_barrier((own, lists))
        parts = own, lax.ppermute(own, "rows", beside_pairs(rows)), distant
        fresh = apply_step(lists, shuffle, parts, arrange(lists, tiles), base, rest, final)
        if final:
            return fresh
        upward = layer == (up_move[1] if up_move else -1)
        down, up = jnp.where(upward, down, fresh), jnp.where(upward, fresh, up)


def solution(mesh):
    return jax.shard_map(
        shards,
        mesh=mesh,
        in_specs=(
            P("layer", None, "rows"),
            P("layer", None, "rows"),
            P("layer", "rows", None, None),
            P("layer", "rows", None, None),
            P("layer", "rows"),
            P("layer", "rows"),
            P(),
        ),
        out_specs=P("layer", None, "rows"),
        check_vma=False,
    )
```

time: 12.9 us -> 10.1 us (0.78)
  the two profiles are of different devices: /device:TPU:31 before, /device:TPU:0 now
where the time goes in v2:
time: 10.1 us; the launch traced here: 9.92 us
  starting transfers between devices  4.29 us (42%)
  Pallas kernels  4.26 us (42%)
  other arithmetic  0.85 us (8%)
  waiting for transfers between devices  0.49 us (5%)
    ppermute x2, starting transfers between devices, exchange(): return (lax.ppermute(block, axes, near), lax.ppermute(block, axes, far))  3.08 us
    pallas_call x1, Pallas kernels, prepare(): pl.pallas_call(functools.partial(prepare_kernel, moves, final), out_shape...  1.77 us
    pallas_call x1, Pallas kernels, apply_step(): pl.pallas_call(kernel, out_shape=jax.ShapeDtypeStruct((1, shots, count *...  1.37 us
    ppermute x1, starting transfers between devices, shards(): parts = (own, lax.ppermute(own, 'rows', beside_pairs(rows)), distant)  1.21 us
    pallas_call x1, Pallas kernels, arrange(): pl.pallas_call(arrange_kernel, out_shape=jax.ShapeDtypeStruct((pairs, 2 *...  1.12 us
    select_n x1, other arithmetic, shards(): leaving = jnp.where(layer == up_move[0], up, down)  0.85 us
    ppermute x2, waiting for transfers between devices, exchange(): return (lax.ppermute(block, axes, near), lax.ppermute(block, axes, far))  0.49 us
  transfers between devices with their start and end apart: 3, of which 2 were waited for; matrix products, arithmetic and copies ran while one was open for 0% of the time, Pallas kernels for 29%

profile of v2, /device:TPU:0, one launch (start us, length us, event | category | flops | bytes accessed | tf_op | source)
XLA Modules:
  0.0 9.9 jit_solution(8613387821323249931)
XLA Ops:
  0.0 0.9 %broadcast_select_fusion = bf16[1,32,1024]{2,1,0:T(8,128)(2,1)S(1)} fusion(bf16[1,32,1024]{2,1,0:T(8,128)(2,1)} %up.1, bf16[1,32,1024]{2,1,0:T(8,128)(2,1)} %down.1, pred[]{:T(512)S(6)} %eq.3), kind=kLoop, calls=%fused_computation | loop fusion | flops 32768 | bytes 196609 | tf_op jit(solution)/shard_map/jit(_where)/select_n | solution.py:244
  0.9 3.0 %collective-permute-start = (bf16[1,32,1024]{2,1,0:T(8,128)(2,1)S(1)}, bf16[1,32,1024]{2,1,0:T(8,128)(2,1)S(1)}, u32[]{:S(2)}, u32[]{:S(2)}) collective-permute-start(bf16[1,32,1024]{2,1,0:T(8,128)(2,1)S(1)} %broadcast_select_fusion), channel_id=1, source_target_pairs={{0,16},{1,17},{2,18},{3,19},{4,20},{5,21},{6,22},{7,23},{8,24},{9,... | collective-permute-start | bytes 196616 | tf_op jit(solution)/shard_map/ppermute | solution.py:40
  3.9 0.1 collective-permute-start.2
  3.9 1.8 %prepare.1 = (bf16[64,128,128]{2,1,0:T(8,128)(2,1)S(1)}, s32[3,36]{1,0:T(4,128)S(1)}, bf16[32,32]{1,0:T(8,128)(2,1)S(1)}, f32[8,32,128]{2,1,0:T(8,128)S(1)}, bf16[8,32,128]{2,1,0:T(8,128)(2,1)S(1)}) custom-call(bf16[1,64,128,128]{3,2,1,0:T(8,128)(2,1)} %down_tiles.1, bf16[1,64,128,128]{3,2,1,0:T(8,128)(2,1)} %up_tiles.1, s32[1,64]{1,0:T(1,128)} %tile_rows.1, ...), custom_call_target="tpu_custom_call" | custom-call | bytes 4194304 | tf_op jit(solution)/shard_map/prepare/pallas_call | solution.py:136
  5.7 0.4 %collective-permute-done.own = bf16[1,32,1024]{2,1,0:T(8,128)(2,1)S(1)} collective-permute-done((bf16[1,32,1024]{2,1,0:T(8,128)(2,1)S(1)}, bf16[1,32,1024]{2,1,0:T(8,128)(2,1)S(1)}, u32[]{:S(2)}, u32[]{:S(2)}) %collective-permute-start) | collective-permute-done | bytes 65568 | tf_op jit(solution)/shard_map/ppermute | solution.py:40
  6.1 1.2 %collective-permute-start.1 = (bf16[1,32,1024]{2,1,0:T(8,128)(2,1)S(1)}, bf16[1,32,1024]{2,1,0:T(8,128)(2,1)S(1)}, u32[]{:S(2)}, u32[]{:S(2)}) collective-permute-start(bf16[1,32,1024]{2,1,0:T(8,128)(2,1)S(1)} %collective-permute-done.own), channel_id=1, source_target_pairs={{0,1},{1,0},{2,3},{3,2},{4,5},{5,4},{6,7},{7,6},{8,9},{9,8},{10,11... | collective-permute-start | bytes 196616 | tf_op jit(solution)/shard_map/ppermute | solution.py:250
  7.3 1.1 %arrange.1.weights = bf16[36,256,128]{2,1,0:T(8,128)(2,1)S(1)} custom-call(s32[3,36]{1,0:T(4,128)S(1)} %get-tuple-element.13.lists, bf16[64,128,128]{2,1,0:T(8,128)(2,1)S(1)} %get-tuple-element.16.tiles), custom_call_target="tpu_custom_call" | custom-call | bytes 4194304 | tf_op jit(solution)/shard_map/arrange/pallas_call | solution.py:172
  8.4 0.1 collective-permute-done.2.distant
  8.5 0.0 collective-permute-done.1.beside
  8.5 1.4 %apply_step.1 = bf16[1,32,1024]{2,1,0:T(8,128)(2,1)} custom-call(s32[3,36]{1,0:T(4,128)S(1)} %get-tuple-element.13.lists, bf16[32,32]{1,0:T(8,128)(2,1)S(1)} %get-tuple-element.14.shuffle, bf16[1,32,1024]{2,1,0:T(8,128)(2,1)S(1)} %collective-permute-done.own, bf16[1,32,1024]{2,1,0:T(8,128)(2,1)S(1)} %collective-permute-done.1.beside, ...), custom_call_target="tpu_custom_call" | custom-call | flops 75497472 | bytes 2359296 | tf_op jit(solution)/shard_map/apply_step/pallas_call | solution.py:213
Async XLA Ops:
  0.9 5.3 %collective-permute-start = (bf16[1,32,1024]{2,1,0:T(8,128)(2,1)S(1)}, bf16[1,32,1024]{2,1,0:T(8,128)(2,1)S(1)}, u32[]{:S(2)}, u32[]{:S(2)}) collective-permute-start(bf16[1,32,1024]{2,1,0:T(8,128)(2,1)S(1)} %broadcast_select_fusion), channel_id=1, source_target_pairs={{0,16},{1,17},{2,18},{3,19},{4,20},{5,21},{6,22},{7,23},{8,24},{9,... | collective-permute-start | bytes 196616 | tf_op jit(solution)/shard_map/ppermute | solution.py:40
  3.9 4.7 %collective-permute-start.2 = (bf16[1,32,1024]{2,1,0:T(8,128)(2,1)S(1)}, bf16[1,32,1024]{2,1,0:T(8,128)(2,1)S(1)}, u32[]{:S(2)}, u32[]{:S(2)}) collective-permute-start(bf16[1,32,1024]{2,1,0:T(8,128)(2,1)S(1)} %broadcast_select_fusion), channel_id=1, source_target_pairs={{0,16},{1,18},{2,17},{3,20},{4,19},{5,22},{6,21},{7,24},{8,23},{9,... | collective-permute-start | bytes 196616 | tf_op jit(solution)/shard_map/ppermute | solution.py:40
  6.1 2.4 %collective-permute-start.1 = (bf16[1,32,1024]{2,1,0:T(8,128)(2,1)S(1)}, bf16[1,32,1024]{2,1,0:T(8,128)(2,1)S(1)}, u32[]{:S(2)}, u32[]{:S(2)}) collective-permute-start(bf16[1,32,1024]{2,1,0:T(8,128)(2,1)S(1)} %collective-permute-done.own), channel_id=1, source_target_pairs={{0,1},{1,0},{2,3},{3,2},{4,5},{5,4},{6,7},{7,6},{8,9},{9,8},{10,11... | collective-permute-start | bytes 196616 | tf_op jit(solution)/shard_map/ppermute | solution.py:250

commit v3 on v1

v3 whole, which is shorter than its diff:
```python
import functools

import jax
import jax.numpy as jnp
from jax import lax
from jax.experimental import pallas as pl
from jax.experimental.pallas import tpu as pltpu
from jax.sharding import PartitionSpec as P

TILE = 128
VMEM_BYTES = 32 * 1024 * 1024


def wavefront(layers):
    steps = []
    for t in range(layers - 1):
        down, up = (t, t + 1), (layers - 1 - t, layers - 2 - t)
        if down[0] == up[0] or down[1] == up[1]:
            steps += [(down, None), (None, up)]
        else:
            steps.append((down, up))
    return steps


def partner(r, rows):
    other = r ^ 1
    return other if other < rows else r


def farther(r, rows):
    other = r + 1 if r % 2 else r - 1
    return other if 0 <= other < rows else r


def across(block, moves, rows):
    moves = [m for m in moves if m is not None]
    axes = ("layer", "rows")
    near = [(s * rows + r, d * rows + partner(r, rows)) for s, d in moves for r in range(rows)]
    far = [(s * rows + r, d * rows + farther(r, rows)) for s, d in moves for r in range(rows)]
    return lax.ppermute(block, axes, near), lax.ppermute(duplicate(block), axes, far)


def duplicate(block):
    def kernel(block, out):
        out[...] = block[...]

    return call(kernel, "duplicate", block, flops=3 * 10**9)(block)


def call(kernel, name, out, scratch=(), flops=0, moved=0):
    vmem = pl.BlockSpec(memory_space=pltpu.VMEM)
    shapes = jax.tree.map(lambda leaf: jax.ShapeDtypeStruct(leaf.shape, leaf.dtype), out)

    def run(*operands):
        return pl.pallas_call(
            kernel,
            out_shape=shapes,
            in_specs=[vmem] * len(operands),
            out_specs=jax.tree.map(lambda _: vmem, shapes),
            scratch_shapes=scratch,
            compiler_params=pltpu.CompilerParams(vmem_limit_bytes=VMEM_BYTES),
            cost_estimate=pl.CostEstimate(flops=flops, bytes_accessed=moved, transcendentals=0),
            name=name,
        )(*operands)

    return run


def roles(moves):
    layer = lax.axis_index("layer")
    down_move, up_move = moves
    upward = layer == (up_move[1] if up_move else -1)
    downward = layer == (down_move[1] if down_move else -1)
    return upward, jnp.logical_or(upward, downward)


def bits(tiles, count):
    return (2 * count).bit_length(), (tiles - 1).bit_length()


def prepare_kernel(moves, final, count, tile_rows, tile_cols, order, lists, shuffle):
    _, active = roles(moves)
    me = lax.axis_index("rows")
    n, shots = tile_rows.shape[1], shuffle.shape[0]
    pairs = lists.shape[1]
    block_bits, tile_bits = bits(n, count)
    even = me % 2 == 0
    row = tile_rows[...] - me * count
    seen = tile_cols[...] - (me - 1) * count
    far_start, beside_start = jnp.where(even, 0, 2 * count), jnp.where(even, 2 * count, 0)
    far = (seen >= far_start) & (seen < far_start + count)
    mine = (seen >= count) & (seen < 2 * count)
    near = jnp.where(mine, seen - count, seen - beside_start + count)
    block = jnp.where(far, seen - far_start, near)
    block = jnp.where(active, block, 2 * count)
    line = row + jnp.where(far, count, 0)

    def both_ways(value):
        wide = jnp.broadcast_to(value.astype(jnp.float32), (n, n))
        return wide, wide.T

    line_l, line_s = both_ways(line)
    block_s = both_ways(block)[1][:, :1]
    t_l = lax.broadcasted_iota(jnp.int32, (n, n), 1)
    t_s = lax.broadcasted_iota(jnp.int32, (n, n), 0)
    same = line_l == line_s
    rank_l = jnp.sum(jnp.where(same & (t_s < t_l), 1.0, 0.0), axis=0, keepdims=True)
    rank_s = jnp.sum(jnp.where(same & (t_l < t_s), 1.0, 0.0), axis=1, keepdims=True)
    half_l, half_s = jnp.floor(rank_l * 0.5), jnp.floor(rank_s * 0.5)
    first_l, first_s = rank_l == 2.0 * half_l, rank_s == 2.0 * half_s
    number = t_s[:, :1].astype(jnp.float32)
    code_s = number * 2**block_bits + block_s
    nothing = 2.0 * count
    slot = lax.broadcasted_iota(jnp.int32, (n, pairs), 1).astype(jnp.float32)

    def listed(hits, value):
        return jnp.sum(jnp.where(hits, value, 0.0), axis=0, keepdims=True)

    for group in range(2):
        low, high = group * count, (group + 1) * count
        member = (line_s[:, :1] >= low) & (line_s[:, :1] < high)
        counted = (line_l >= low) & (line_l < line_s) & first_l
        ahead = jnp.sum(jnp.where(counted, 1.0, 0.0), axis=1, keepdims=True)
        hit = (ahead + half_s == slot) & member
        hit_a, hit_b = hit & first_s, hit & jnp.logical_not(first_s)
        here = (line_s[:, :1] - low) * 2 ** (block_bits + tile_bits)
        word_a = listed(hit_a, here + code_s - nothing) + nothing
        word_b = listed(hit_b, code_s - nothing) + nothing
        lists[2 * group : 2 * group + 1, :] = word_a.astype(jnp.int32)
        lists[2 * group + 1 : 2 * group + 2, :] = word_b.astype(jnp.int32)
        used = jnp.sum(listed(hit_a, jnp.ones_like(number)), axis=1, keepdims=True)
    lists[4:5, :] = jnp.broadcast_to(used.astype(jnp.int32), (1, pairs))

    slots = lax.broadcasted_iota(jnp.int32, (shots, shots), 0)
    wanted = order[...] if final else lax.broadcasted_iota(jnp.int32, (shots, shots), 1)
    shuffle[...] = (slots == wanted).astype(jnp.float32).T.astype(jnp.bfloat16)


def arrange_kernel(moves, down_tiles, up_tiles, weights):
    rows = lax.broadcasted_iota(jnp.int32, (TILE, TILE), 0)
    identity = (rows == lax.broadcasted_iota(jnp.int32, (TILE, TILE), 1)).astype(jnp.bfloat16)
    upward, _ = roles(moves)

    def lay(tiles):
        for t in range(weights.shape[0]):
            if t % 2:
                weights[t] = lax.dot_general(
                    identity, tiles[0, t], (((1,), (1,)), ((), ())), preferred_element_type=jnp.float32
                ).astype(jnp.bfloat16)
            else:
                weights[t] = tiles[0, t].T

    pl.when(upward)(lambda: lay(up_tiles))
    pl.when(jnp.logical_not(upward))(lambda: lay(down_tiles))


def add_products(lists, group, pairs, blocks, weights, total):
    block_bits, tile_bits = bits(weights.shape[0], total.shape[0])
    block_mask, tile_mask = 2**block_bits - 1, 2**tile_bits - 1
    for p in range(*pairs):
        a, b = lists[2 * group, p], lists[2 * group + 1, p]
        read = jnp.concatenate([blocks[a & block_mask], blocks[b & block_mask]], axis=1)
        tile_a, tile_b = (a >> block_bits) & tile_mask, b >> block_bits
        both = jnp.concatenate([weights[tile_a], weights[tile_b]], axis=0)
        row = a >> (block_bits + tile_bits)
        total[row] += jnp.dot(read, both, preferred_element_type=jnp.float32)


def near_kernel(moves, lists, own, beside, weights, down, up, total, blocks):
    count, shots = total.shape[0], total.shape[1]
    upward, _ = roles(moves)
    for k in range(count):
        here = slice(k * TILE, (k + 1) * TILE)
        blocks[k] = own[0, :, here]
        blocks[count + k] = beside[0, :, here]
        total[k] = jnp.where(upward, up[0, :, here], down[0, :, here]).astype(jnp.float32)
    blocks[2 * count] = jnp.zeros((shots, TILE), jnp.bfloat16)
    add_products(lists, 0, (0, lists.shape[1]), blocks, weights, total)


def far_kernel(moves, final, lists, shuffle, distant, weights, near_total, down, up, out, blocks, total):
    count, shots = total.shape[0], total.shape[1]
    upward, _ = roles(moves)
    for k in range(count):
        blocks[k] = distant[0, :, k * TILE:(k + 1) * TILE]
    blocks[2 * count] = jnp.zeros((shots, TILE), jnp.bfloat16)
    total[...] = near_total[...]
    pairs = lists.shape[1]
    usual, most = -(-pairs // 3), -(-4 * pairs // 9)
    used = lists[4, 0]
    add_products(lists, 1, (0, usual), blocks, weights, total)
    pl.when(used > usual)(lambda: add_products(lists, 1, (usual, most), blocks, weights, total))
    pl.when(used > most)(lambda: add_products(lists, 1, (most, pairs), blocks, weights, total))
    for k in range(count):
        here = slice(k * TILE, (k + 1) * TILE)
        fresh = total[k].astype(jnp.bfloat16)
        if final:
            rest = jnp.where(upward, down[0, :, here], up[0, :, here])
            fresh = (fresh.astype(jnp.float32) + rest.astype(jnp.float32)).astype(jnp.bfloat16)
        fresh = jnp.dot(shuffle[...], fresh, preferred_element_type=jnp.float32)
        out[0, :, here] = fresh.astype(jnp.bfloat16)


def step(moves, final, leaving, down, up, down_tiles, up_tiles, tile_rows, tile_cols, order):
    rows = lax.axis_size("rows")
    _, shots, width = down.shape
    tiles, count = tile_rows.shape[1], width // TILE
    pairs = (tiles + min(tiles, count)) // 2
    shape = jax.ShapeDtypeStruct
    sums = shape((count, shots, TILE), jnp.float32)
    blocks = pltpu.VMEM((2 * count + 1, shots, TILE), jnp.bfloat16)

    beside, distant = across(leaving, moves, rows)
    lists, shuffle = call(
        functools.partial(prepare_kernel, moves, final, count),
        "prepare",
        (shape((5, pairs), jnp.int32), shape((shots, shots), jnp.bfloat16)),
    )(tile_rows, tile_cols, order)
    beside, lists = lax.optimization_barrier((beside, lists))
    own = lax.ppermute(beside, "rows", [(r, partner(r, rows)) for r in range(rows)])
    weights = call(
        functools.partial(arrange_kernel, moves),
        "arrange",
        shape((tiles, TILE, TILE), down_tiles.dtype),
        flops=3 * 10**9,
    )(down_tiles, up_tiles)
    total = call(functools.partial(near_kernel, moves), "near", sums, [blocks])(
        lists, own, beside, weights, down, up
    )
    return call(
        functools.partial(far_kernel, moves, final),
        "far",
        down,
        [blocks, pltpu.VMEM(sums.shape, sums.dtype)],
    )(lists, shuffle, distant, weights, total, down, up)


def shards(down_sources, up_sources, down_tiles, up_tiles, tile_rows, tile_cols, shot_order):
    layer = lax.axis_index("layer")
    order = shot_order.reshape(1, -1)
    steps = wavefront(lax.axis_size("layer"))
    down, up = down_sources, up_sources
    for at, moves in enumerate(steps):
        down_move, up_move = moves
        if up_move is None:
            leaving = down
        elif down_move is None:
            leaving = up
        else:
            leaving = jnp.where(layer == up_move[0], up, down)
        final = at == len(steps) - 1
        fresh = step(
            moves, final, leaving, down, up, down_tiles, up_tiles, tile_rows, tile_cols, order
        )
        if final:
            return fresh
        upward, _ = roles(moves)
        down, up = jnp.where(upward, down, fresh), jnp.where(upward, fresh, up)


def solution(mesh):
    return jax.shard_map(
        shards,
        mesh=mesh,
        in_specs=(
            P("layer", None, "rows"),
            P("layer", None, "rows"),
            P("layer", "rows", None, None),
            P("layer", "rows", None, None),
            P("layer", "rows"),
            P("layer", "rows"),
            P(),
        ),
        out_specs=P("layer", None, "rows"),
        check_vma=False,
    )
```

time: 12.9 us -> 9.75 us (0.76)
  the two profiles are of different devices: /device:TPU:31 before, /device:TPU:27 now
where the time goes in v3:
time: 9.75 us; the launch traced here: 9.56 us
  starting transfers between devices  3.16 us (32%)
  Pallas kernels  2.92 us (30%)
  waiting for transfers between devices  2.52 us (26%)
  other arithmetic  0.85 us (9%)
    pallas_call x5, Pallas kernels, run(): pl.pallas_call(kernel, out_shape=shapes, in_specs=[vmem] * len(operands),...  2.92 us
    ppermute x1, starting transfers between devices, across(): lax.ppermute(duplicate(block), axes, far)  1.89 us
    ppermute x1, waiting for transfers between devices, across(): lax.ppermute(block, axes, near)  1.62 us
    ppermute x1, starting transfers between devices, across(): lax.ppermute(block, axes, near)  0.88 us
    ppermute x1, waiting for transfers between devices, across(): lax.ppermute(duplicate(block), axes, far)  0.86 us
    select_n x1, other arithmetic, shards(): leaving = jnp.where(layer == up_move[0], up, down)  0.85 us
    ppermute x1, starting transfers between devices, step(): lax.ppermute(beside, 'rows', [(r, partner(r, rows)) for r in range(rows)])  0.39 us
  transfers between devices with their start and end apart: 3, of which 2 were waited for; matrix products, arithmetic and copies ran while one was open for 0% of the time, Pallas kernels for 19%

profile of v3, /device:TPU:27, one launch (start us, length us, event | category | flops | bytes accessed | tf_op | source)
XLA Modules:
  0.0 9.6 jit_solution(15558876419552822517)
XLA Ops:
  0.0 0.9 %broadcast_select_fusion.block = bf16[1,32,1024]{2,1,0:T(8,128)(2,1)S(1)} fusion(bf16[1,32,1024]{2,1,0:T(8,128)(2,1)} %up.3, bf16[1,32,1024]{2,1,0:T(8,128)(2,1)} %down.3, pred[]{:T(512)S(6)} %eq.3), kind=kLoop, calls=%fused_computation | loop fusion | flops 32768 | bytes 196609 | tf_op jit(solution)/shard_map/jit(_where)/select_n | solution.py:250
  0.9 0.0 copy-start.4
  0.9 0.0 copy-start.5
  0.9 0.0 copy-start.6
  0.9 0.0 copy-start.2
  0.9 0.0 copy-start.3
  0.9 0.9 %collective-permute-start = (bf16[1,32,1024]{2,1,0:T(8,128)(2,1)S(1)}, bf16[1,32,1024]{2,1,0:T(8,128)(2,1)S(1)}, u32[]{:S(2)}, u32[]{:S(2)}) collective-permute-start(bf16[1,32,1024]{2,1,0:T(8,128)(2,1)S(1)} %broadcast_select_fusion.block), channel_id=1, source_target_pairs={{0,17},{1,16},{2,19},{3,18},{4,21},{5,20},{6,23},{7,22},{8,25},{9,... | collective-permute-start | bytes 196616 | tf_op jit(solution)/shard_map/ppermute | solution.py:40
  1.8 1.9 %collective-permute-start.1 = (bf16[1,32,1024]{2,1,0:T(8,128)(2,1)S(1)}, bf16[1,32,1024]{2,1,0:T(8,128)(2,1)S(1)}, u32[]{:S(2)}, u32[]{:S(2)}) collective-permute-start(bf16[1,32,1024]{2,1,0:T(8,128)(2,1)S(1)} %duplicate.1), channel_id=1, source_target_pairs={{0,16},{1,18},{2,17},{3,20},{4,19},{5,22},{6,21},{7,24},{8,23},{9,... | collective-permute-start | bytes 196616 | tf_op jit(solution)/shard_map/ppermute | solution.py:40
  3.7 0.0 copy-done.4
  3.7 0.0 copy-done.5
  3.7 0.0 copy-done.6
  3.7 0.3 %prepare.1 = (s32[5,36]{1,0:T(8,128)S(1)}, bf16[32,32]{1,0:T(8,128)(2,1)S(1)}) custom-call(s32[1,64]{1,0:T(1,128)S(1)} %copy-done.4, s32[1,64]{1,0:T(1,128)S(1)} %copy-done.5, s32[1,32]{1,0:T(1,128)S(1)} %bitcast.1), custom_call_target="tpu_custom_call" | custom-call | tf_op jit(solution)/shard_map/prepare/pallas_call | solution.py:55
  4.0 1.6 %collective-permute-done.beside = bf16[1,32,1024]{2,1,0:T(8,128)(2,1)S(1)} collective-permute-done((bf16[1,32,1024]{2,1,0:T(8,128)(2,1)S(1)}, bf16[1,32,1024]{2,1,0:T(8,128)(2,1)S(1)}, u32[]{:S(2)}, u32[]{:S(2)}) %collective-permute-start) | collective-permute-done | bytes 65568 | tf_op jit(solution)/shard_map/ppermute | solution.py:40
  5.6 0.0 copy-start
  5.6 0.0 copy-start.1
  5.6 0.4 %collective-permute-start.2 = (bf16[1,32,1024]{2,1,0:T(8,128)(2,1)S(1)}, bf16[1,32,1024]{2,1,0:T(8,128)(2,1)S(1)}, u32[]{:S(2)}, u32[]{:S(2)}) collective-permute-start(bf16[1,32,1024]{2,1,0:T(8,128)(2,1)S(1)} %collective-permute-done.beside), channel_id=1, source_target_pairs={{0,1},{1,0},{2,3},{3,2},{4,5},{5,4},{6,7},{7,6},{8,9},{9,8},{10,11... | collective-permute-start | bytes 196616 | tf_op jit(solution)/shard_map/ppermute | solution.py:220
  6.0 0.0 copy-done.2
  6.0 0.0 copy-done.3
  6.0 0.8 %arrange.1.weights = bf16[64,128,128]{2,1,0:T(8,128)(2,1)S(1)} custom-call(bf16[1,64,128,128]{3,2,1,0:T(8,128)(2,1)S(1)} %copy-done.2, bf16[1,64,128,128]{3,2,1,0:T(8,128)(2,1)S(1)} %copy-done.3), custom_call_target="tpu_custom_call" | custom-call | flops 3000000000 | tf_op jit(solution)/shard_map/arrange/pallas_call | solution.py:55
  6.9 0.0 collective-permute-done.2.own
  6.9 0.0 copy-done
  6.9 0.0 copy-done.1
  6.9 0.6 %near.1.near_total = f32[8,32,128]{2,1,0:T(8,128)S(1)} custom-call(s32[5,36]{1,0:T(8,128)S(1)} %get-tuple-element.10.lists, bf16[1,32,1024]{2,1,0:T(8,128)(2,1)S(1)} %collective-permute-done.2.own, bf16[1,32,1024]{2,1,0:T(8,128)(2,1)S(1)} %collective-permute-done.beside, bf16[64,128,128]{2,1,0:T(8,128)(2,1)S(1)} %arrange.1.weights, ...), custom_call_target="tpu_custom_call" | custom-call | tf_op jit(solution)/shard_map/near/pallas_call | solution.py:55
  7.6 0.9 %collective-permute-done.1.distant = bf16[1,32,1024]{2,1,0:T(8,128)(2,1)S(1)} collective-permute-done((bf16[1,32,1024]{2,1,0:T(8,128)(2,1)S(1)}, bf16[1,32,1024]{2,1,0:T(8,128)(2,1)S(1)}, u32[]{:S(2)}, u32[]{:S(2)}) %collective-permute-start.1) | collective-permute-done | bytes 65568 | tf_op jit(solution)/shard_map/ppermute | solution.py:40
  8.4 1.1 %far.1 = bf16[1,32,1024]{2,1,0:T(8,128)(2,1)} custom-call(s32[5,36]{1,0:T(8,128)S(1)} %get-tuple-element.10.lists, bf16[32,32]{1,0:T(8,128)(2,1)S(1)} %get-tuple-element.11.shuffle, bf16[1,32,1024]{2,1,0:T(8,128)(2,1)S(1)} %collective-permute-done.1.distant, bf16[64,128,128]{2,1,0:T(8,128)(2,1)S(1)} %arrange.1.weights, f32[8,32,128]{2,1,0:T(8,128)S(1)} %near.1.near_total, ...), custom_call_target="tpu_custom_call" | custom-call | tf_op jit(solution)/shard_map/far/pallas_call | solution.py:55
  (1 shorter events, 0.0 us)
Async XLA Ops:
  0.9 2.8 %copy-start.4 = (s32[1,64]{1,0:T(1,128)S(1)}, s32[1,64]{1,0:T(1,128)}, u32[]{:S(2)}) copy-start(s32[1,64]{1,0:T(1,128)} %tile_rows.1) | copy-start | bytes 772
  0.9 2.8 %copy-start.5 = (s32[1,64]{1,0:T(1,128)S(1)}, s32[1,64]{1,0:T(1,128)}, u32[]{:S(2)}) copy-start(s32[1,64]{1,0:T(1,128)} %tile_cols.1) | copy-start | bytes 772
  0.9 2.8 %copy-start.6 = (s32[32]{0:T(128)S(1)}, s32[32]{0:T(128)}, u32[]{:S(2)}) copy-start(s32[32]{0:T(128)} %param.13) | copy-start | bytes 388
  0.9 5.1 %copy-start.2 = (bf16[1,64,128,128]{3,2,1,0:T(8,128)(2,1)S(1)}, bf16[1,64,128,128]{3,2,1,0:T(8,128)(2,1)}, u32[]{:S(2)}) copy-start(bf16[1,64,128,128]{3,2,1,0:T(8,128)(2,1)} %down_tiles.1) | copy-start | bytes 6291460
  0.9 5.1 %copy-start.3 = (bf16[1,64,128,128]{3,2,1,0:T(8,128)(2,1)S(1)}, bf16[1,64,128,128]{3,2,1,0:T(8,128)(2,1)}, u32[]{:S(2)}) copy-start(bf16[1,64,128,128]{3,2,1,0:T(8,128)(2,1)} %up_tiles.1) | copy-start | bytes 6291460
  0.9 4.7 %collective-permute-start = (bf16[1,32,1024]{2,1,0:T(8,128)(2,1)S(1)}, bf16[1,32,1024]{2,1,0:T(8,128)(2,1)S(1)}, u32[]{:S(2)}, u32[]{:S(2)}) collective-permute-start(bf16[1,32,1024]{2,1,0:T(8,128)(2,1)S(1)} %broadcast_select_fusion.block), channel_id=1, source_target_pairs={{0,17},{1,16},{2,19},{3,18},{4,21},{5,20},{6,23},{7,22},{8,25},{9,... | collective-permute-start | bytes 196616 | tf_op jit(solution)/shard_map/ppermute | solution.py:40
  1.8 6.6 %collective-permute-start.1 = (bf16[1,32,1024]{2,1,0:T(8,128)(2,1)S(1)}, bf16[1,32,1024]{2,1,0:T(8,128)(2,1)S(1)}, u32[]{:S(2)}, u32[]{:S(2)}) collective-permute-start(bf16[1,32,1024]{2,1,0:T(8,128)(2,1)S(1)} %duplicate.1), channel_id=1, source_target_pairs={{0,16},{1,18},{2,17},{3,20},{4,19},{5,22},{6,21},{7,24},{8,23},{9,... | collective-permute-start | bytes 196616 | tf_op jit(solution)/shard_map/ppermute | solution.py:40
  5.6 1.3 %copy-start = (bf16[1,32,1024]{2,1,0:T(8,128)(2,1)S(1)}, bf16[1,32,1024]{2,1,0:T(8,128)(2,1)}, u32[]{:S(2)}) copy-start(bf16[1,32,1024]{2,1,0:T(8,128)(2,1)} %up.3) | copy-start | bytes 196612
  5.6 1.3 %copy-start.1 = (bf16[1,32,1024]{2,1,0:T(8,128)(2,1)S(1)}, bf16[1,32,1024]{2,1,0:T(8,128)(2,1)}, u32[]{:S(2)}) copy-start(bf16[1,32,1024]{2,1,0:T(8,128)(2,1)} %down.3) | copy-start | bytes 196612
  5.6 1.3 %collective-permute-start.2 = (bf16[1,32,1024]{2,1,0:T(8,128)(2,1)S(1)}, bf16[1,32,1024]{2,1,0:T(8,128)(2,1)S(1)}, u32[]{:S(2)}, u32[]{:S(2)}) collective-permute-start(bf16[1,32,1024]{2,1,0:T(8,128)(2,1)S(1)} %collective-permute-done.beside), channel_id=1, source_target_pairs={{0,1},{1,0},{2,3},{3,2},{4,5},{5,4},{6,7},{7,6},{8,9},{9,8},{10,11... | collective-permute-start | bytes 196616 | tf_op jit(solution)/shard_map/ppermute | solution.py:220

commit v4 on v3

v4 whole, which is shorter than its diff:
```python
import functools

import jax
import jax.numpy as jnp
from jax import lax
from jax.experimental import pallas as pl
from jax.experimental.pallas import tpu as pltpu
from jax.sharding import PartitionSpec as P

TILE = 128
VMEM_BYTES = 32 * 1024 * 1024


def wavefront(layers):
    steps = []
    for t in range(layers - 1):
        down, up = (t, t + 1), (layers - 1 - t, layers - 2 - t)
        if down[0] == up[0] or down[1] == up[1]:
            steps += [(down, None), (None, up)]
        else:
            steps.append((down, up))
    return steps


def partner(r, rows):
    other = r ^ 1
    return other if other < rows else r


def farther(r, rows):
    other = r + 1 if r % 2 else r - 1
    return other if 0 <= other < rows else r


def crosses(r):
    return r < 2


def across(block, moves, rows):
    moves = [m for m in moves if m is not None]
    axes = ("layer", "rows")
    first = [partner(r, rows) if crosses(r) else r for r in range(rows)]
    near = [(s * rows + r, d * rows + first[r]) for s, d in moves for r in range(rows)]
    far = [(s * rows + r, d * rows + farther(r, rows)) for s, d in moves for r in range(rows)]
    return lax.ppermute(block, axes, near), lax.ppermute(duplicate(block), axes, far)


def duplicate(block):
    def kernel(block, out):
        out[...] = block[...]

    return call(kernel, "duplicate", block, flops=3 * 10**9)(block)


def call(kernel, name, out, scratch=(), flops=0):
    vmem = pl.BlockSpec(memory_space=pltpu.VMEM)
    shapes = jax.tree.map(lambda leaf: jax.ShapeDtypeStruct(leaf.shape, leaf.dtype), out)

    def run(*operands):
        return pl.pallas_call(
            kernel,
            out_shape=shapes,
            in_specs=[vmem] * len(operands),
            out_specs=jax.tree.map(lambda _: vmem, shapes),
            scratch_shapes=scratch,
            compiler_params=pltpu.CompilerParams(vmem_limit_bytes=VMEM_BYTES),
            cost_estimate=pl.CostEstimate(flops=flops, bytes_accessed=0, transcendentals=0),
            name=name,
        )(*operands)

    return run


def roles(moves):
    layer = lax.axis_index("layer")
    down_move, up_move = moves
    upward = layer == (up_move[1] if up_move else -1)
    downward = layer == (down_move[1] if down_move else -1)
    return upward, jnp.logical_or(upward, downward)


def bits(tiles, count):
    return count.bit_length(), (tiles - 1).bit_length()


def prepare_kernel(
    moves, count, tile_rows, tile_cols, order, down_tiles, up_tiles, lists, source, weights
):
    arrange(moves, down_tiles, up_tiles, weights)
    _, active = roles(moves)
    me = lax.axis_index("rows")
    n, shots = tile_rows.shape[1], source.shape[0]
    pairs = lists.shape[1]
    column_bits, tile_bits = bits(n, count)
    even = me % 2 == 0
    row = tile_rows[...] - me * count
    seen = tile_cols[...] - (me - 1) * count
    far_start, beside_start = jnp.where(even, 0, 2 * count), jnp.where(even, 2 * count, 0)
    first_start = jnp.where(crosses(me), beside_start, count)
    far = (seen >= far_start) & (seen < far_start + count)
    first = (seen >= first_start) & (seen < first_start + count)
    group = jnp.where(far, 2, jnp.where(first, 0, 1))
    column = seen - jnp.where(seen < count, 0, jnp.where(seen < 2 * count, count, 2 * count))
    column = jnp.where(active, column, count)
    line = row + group * count

    def both_ways(value):
        wide = jnp.broadcast_to(value.astype(jnp.float32), (n, n))
        return wide, wide.T

    line_l, line_s = both_ways(line)
    column_s = both_ways(column)[1][:, :1]
    t_l = lax.broadcasted_iota(jnp.int32, (n, n), 1)
    t_s = lax.broadcasted_iota(jnp.int32, (n, n), 0)
    same = line_l == line_s
    rank_l = jnp.sum(jnp.where(same & (t_s < t_l), 1.0, 0.0), axis=0, keepdims=True)
    rank_s = jnp.sum(jnp.where(same & (t_l < t_s), 1.0, 0.0), axis=1, keepdims=True)
    half_l, half_s = jnp.floor(rank_l * 0.5), jnp.floor(rank_s * 0.5)
    first_l, first_s = rank_l == 2.0 * half_l, rank_s == 2.0 * half_s
    number = t_s[:, :1].astype(jnp.float32)
    code_s = number * 2**column_bits + column_s
    nothing = float(count)
    slot = lax.broadcasted_iota(jnp.int32, (n, pairs), 1).astype(jnp.float32)

    def listed(hits, value):
        return jnp.sum(jnp.where(hits, value, 0.0), axis=0, keepdims=True)

    for group in range(3):
        low, high = group * count, (group + 1) * count
        member = (line_s[:, :1] >= low) & (line_s[:, :1] < high)
        counted = (line_l >= low) & (line_l < line_s) & first_l
        ahead = jnp.sum(jnp.where(counted, 1.0, 0.0), axis=1, keepdims=True)
        hit = (ahead + half_s == slot) & member
        hit_a, hit_b = hit & first_s, hit & jnp.logical_not(first_s)
        here = (line_s[:, :1] - low) * 2 ** (column_bits + tile_bits)
        word_a = listed(hit_a, here + code_s - nothing) + nothing
        word_b = listed(hit_b, code_s - nothing) + nothing
        used = jnp.sum(listed(hit_a, jnp.ones_like(number)), axis=1, keepdims=True)
        for k, entry in enumerate((word_a, word_b, jnp.broadcast_to(used, (1, pairs)))):
            lists[3 * group + k : 3 * group + k + 1, :] = entry.astype(jnp.int32)

    wide = jnp.broadcast_to(order[...].astype(jnp.float32), (shots, shots))
    source[...] = jnp.broadcast_to(wide.T[:, :1], source.shape).astype(jnp.int32)


def picked_rows(value, source):
    groups = value.shape[0] // 8
    parts = []
    for i in range(groups):
        want = source[8 * i : 8 * i + 8]
        part = None
        for j in range(groups):
            found = jnp.take_along_axis(value[8 * j : 8 * j + 8], want & 7, axis=0)
            part = found if part is None else jnp.where(want >> 3 == j, found, part)
        parts.append(part)
    return jnp.concatenate(parts, axis=0)


def arrange(moves, down_tiles, up_tiles, weights):
    rows = lax.broadcasted_iota(jnp.int32, (TILE, TILE), 0)
    identity = (rows == lax.broadcasted_iota(jnp.int32, (TILE, TILE), 1)).astype(jnp.bfloat16)
    upward, _ = roles(moves)

    for t in range(weights.shape[0]):
        tile = jnp.where(upward, up_tiles[0, t], down_tiles[0, t])
        if t % 2:
            weights[t] = lax.dot_general(
                identity, tile, (((1,), (1,)), ((), ())), preferred_element_type=jnp.float32
            ).astype(jnp.bfloat16)
        else:
            weights[t] = tile.T


def split(block, columns):
    count = columns.shape[0] - 1
    for k in range(count):
        columns[k] = block[0, :, k * TILE:(k + 1) * TILE]
    columns[count] = jnp.zeros(columns.shape[1:], columns.dtype)


def add_products(lists, group, pairs, columns, weights, total):
    column_bits, tile_bits = bits(weights.shape[0], total.shape[0])
    column_mask, tile_mask = 2**column_bits - 1, 2**tile_bits - 1
    for p in range(*pairs):
        a, b = lists[3 * group, p], lists[3 * group + 1, p]
        read = jnp.concatenate([columns[a & column_mask], columns[b & column_mask]], axis=1)
        tile_a, tile_b = (a >> column_bits) & tile_mask, b >> column_bits
        both = jnp.concatenate([weights[tile_a], weights[tile_b]], axis=0)
        row = a >> (column_bits + tile_bits)
        total[row] += jnp.dot(read, both, preferred_element_type=jnp.float32)


def stage_kernel(moves, final, group, lists, source, block, weights, before, down, up, out, columns, total):
    count, pairs = total.shape[0], lists.shape[1]
    upward, _ = roles(moves)
    split(block, columns)
    for k in range(count):
        here = slice(k * TILE, (k + 1) * TILE)
        if before is None:
            total[k] = jnp.where(upward, up[0, :, here], down[0, :, here]).astype(jnp.float32)
        else:
            total[k] = before[k]

    def finish():
        for k in range(count):
            here = slice(k * TILE, (k + 1) * TILE)
            if group < 2:
                out[k] = total[k]
                continue
            fresh = total[k].astype(jnp.bfloat16)
            if final:
                rest = jnp.where(upward, down[0, :, here], up[0, :, here])
                both = (fresh.astype(jnp.float32) + rest.astype(jnp.float32)).astype(jnp.bfloat16)
                fresh = picked_rows(both.astype(jnp.float32), source[...]).astype(jnp.bfloat16)
            out[0, :, here] = fresh

    def run(*ends):
        add_products(lists, group, (0, ends[0]), columns, weights, total)
        finish()
        for low, high in zip(ends, ends[1:]):

            @pl.when(lists[3 * group + 2, 0] > low)
            def _(low=low, high=high):
                add_products(lists, group, (low, high), columns, weights, total)
                finish()

    some, many = -(-4 * pairs // 9), -(-7 * pairs // 9)
    if group == 0:
        run(pairs)
    elif group == 1:
        own_later = crosses(lax.axis_index("rows"))
        pl.when(own_later)(lambda: run(many, pairs))
        pl.when(jnp.logical_not(own_later))(lambda: run(some, pairs))
    else:
        run(some, pairs)


def step(moves, final, leaving, down, up, down_tiles, up_tiles, tile_rows, tile_cols, order):
    rows = lax.axis_size("rows")
    _, shots, width = down.shape
    tiles, count = tile_rows.shape[1], width // TILE
    pairs = (tiles + min(tiles, count)) // 2
    shape = jax.ShapeDtypeStruct
    sums = shape((count, shots, TILE), jnp.float32)
    scratch = [pltpu.VMEM((count + 1, shots, TILE), jnp.bfloat16), pltpu.VMEM(sums.shape, sums.dtype)]

    first, distant = across(leaving, moves, rows)
    lists, source, weights = call(
        functools.partial(prepare_kernel, moves, count),
        "prepare",
        (
            shape((9, pairs), jnp.int32),
            shape((shots, TILE), jnp.int32),
            shape((tiles, TILE, TILE), down_tiles.dtype),
        ),
    )(tile_rows, tile_cols, order, down_tiles, up_tiles)
    first, lists = lax.optimization_barrier((first, lists))
    second = lax.ppermute(first, "rows", [(r, partner(r, rows)) for r in range(rows)])

    def stage(group, block, before):
        def kernel(lists, source, block, weights, down, up, *others):
            before, others = (None, others) if group == 0 else (others[0], others[1:])
            stage_kernel(moves, final, group, lists, source, block, weights, before, down, up, *others)

        return call(
            kernel,
            ("first", "second", "far")[group],
            down if group == 2 else sums,
            scratch,
            flops=3 * 10**9 if group == 0 else 0,
        )(lists, source, block, weights, down, up, *([] if before is None else [before]))

    total = stage(0, first, None)
    total = stage(1, second, total)
    return stage(2, distant, total)


def shards(down_sources, up_sources, down_tiles, up_tiles, tile_rows, tile_cols, shot_order):
    layer = lax.axis_index("layer")
    order = shot_order.reshape(1, -1)
    steps = wavefront(lax.axis_size("layer"))
    down, up = down_sources, up_sources
    for at, moves in enumerate(steps):
        down_move, up_move = moves
        if up_move is None:
            leaving = down
        elif down_move is None:
            leaving = up
        else:
            leaving = jnp.where(layer == up_move[0], up, down)
        final = at == len(steps) - 1
        fresh = step(
            moves, final, leaving, down, up, down_tiles, up_tiles, tile_rows, tile_cols, order
        )
        if final:
            return fresh
        upward, _ = roles(moves)
        down, up = jnp.where(upward, down, fresh), jnp.where(upward, fresh, up)


def solution(mesh):
    return jax.shard_map(
        shards,
        mesh=mesh,
        in_specs=(
            P("layer", None, "rows"),
            P("layer", None, "rows"),
            P("layer", "rows", None, None),
            P("layer", "rows", None, None),
            P("layer", "rows"),
            P("layer", "rows"),
            P(),
        ),
        out_specs=P("layer", None, "rows"),
        check_vma=False,
    )
```

time: 9.75 us -> 9.52 us (0.976)
  the two profiles are of different devices: /device:TPU:27 before, /device:TPU:31 now
where the time goes in v4:
time: 9.52 us; the launch traced here: 9.34 us
  starting transfers between devices  4.2 us (44%)
  Pallas kernels  3.28 us (34%)
  other arithmetic  0.85 us (9%)
  local copies, waits for them, and re-layouts  0.67 us (7%)
  waiting for transfers between devices  0.27 us (3%)
    pallas_call x5, Pallas kernels, run(): pl.pallas_call(kernel, out_shape=shapes, in_specs=[vmem] * len(operands),...  3.28 us
    ppermute x1, starting transfers between devices, step(): lax.ppermute(first, 'rows', [(r, partner(r, rows)) for r in range(rows)])  2.66 us
    ppermute x1, starting transfers between devices, across(): lax.ppermute(duplicate(block), axes, far)  1.21 us
    select_n x1, other arithmetic, shards(): leaving = jnp.where(layer == up_move[0], up, down)  0.85 us
    unnamed x14, local copies, waits for them, and re-layouts  0.67 us
    ppermute x1, starting transfers between devices, across(): lax.ppermute(block, axes, near)  0.32 us
    ppermute x1, waiting for transfers between devices, step(): lax.ppermute(first, 'rows', [(r, partner(r, rows)) for r in range(rows)])  0.26 us
  transfers between devices with their start and end apart: 3, of which 1 were waited for; matrix products, arithmetic and copies ran while one was open for 0% of the time, Pallas kernels for 23%

profile of v4, /device:TPU:31, one launch (start us, length us, event | category | flops | bytes accessed | tf_op | source)
XLA Modules:
  0.0 9.3 jit_solution(17838086896918852558)
XLA Ops:
  0.0 0.9 %broadcast_select_fusion.block = bf16[1,32,1024]{2,1,0:T(8,128)(2,1)S(1)} fusion(bf16[1,32,1024]{2,1,0:T(8,128)(2,1)} %up.5, bf16[1,32,1024]{2,1,0:T(8,128)(2,1)} %down.5, pred[]{:T(512)S(6)} %eq.3), kind=kLoop, calls=%fused_computation | loop fusion | flops 32768 | bytes 196609 | tf_op jit(solution)/shard_map/jit(_where)/select_n | solution.py:290
  0.9 0.0 copy-start
  0.9 0.0 copy-start.1
  0.9 0.0 copy-start.4
  0.9 0.0 copy-start.5
  0.9 0.0 copy-start.6
  0.9 0.3 %collective-permute-start = (bf16[1,32,1024]{2,1,0:T(8,128)(2,1)S(1)}, bf16[1,32,1024]{2,1,0:T(8,128)(2,1)S(1)}, u32[]{:S(2)}, u32[]{:S(2)}) collective-permute-start(bf16[1,32,1024]{2,1,0:T(8,128)(2,1)S(1)} %broadcast_select_fusion.block), channel_id=1, source_target_pairs={{0,17},{1,16},{2,18},{3,19},{4,20},{5,21},{6,22},{7,23},{8,24},{9,... | collective-permute-start | bytes 196616 | tf_op jit(solution)/shard_map/ppermute | solution.py:45
  1.2 1.2 %collective-permute-start.1 = (bf16[1,32,1024]{2,1,0:T(8,128)(2,1)S(1)}, bf16[1,32,1024]{2,1,0:T(8,128)(2,1)S(1)}, u32[]{:S(2)}, u32[]{:S(2)}) collective-permute-start(bf16[1,32,1024]{2,1,0:T(8,128)(2,1)S(1)} %duplicate.1), channel_id=1, source_target_pairs={{0,16},{1,18},{2,17},{3,20},{4,19},{5,22},{6,21},{7,24},{8,23},{9,... | collective-permute-start | bytes 196616 | tf_op jit(solution)/shard_map/ppermute | solution.py:45
  2.5 0.0 copy-done
  2.5 0.6 %copy-done.1 = bf16[1,64,128,128]{3,2,1,0:T(8,128)(2,1)S(1)} copy-done((bf16[1,64,128,128]{3,2,1,0:T(8,128)(2,1)S(1)}, bf16[1,64,128,128]{3,2,1,0:T(8,128)(2,1)}, u32[]{:S(2)}) %copy-start.1) | copy-done | bytes 2097176
  3.1 0.0 copy-done.4
  3.1 0.0 copy-done.5
  3.1 0.0 copy-done.6
  3.1 0.0 copy-start.2
  3.1 0.0 copy-start.3
  3.1 1.1 %prepare.1 = (s32[9,36]{1,0:T(8,128)S(1)}, s32[32,128]{1,0:T(8,128)S(1)}, bf16[64,128,128]{2,1,0:T(8,128)(2,1)S(1)}) custom-call(s32[1,64]{1,0:T(1,128)S(1)} %copy-done.4, s32[1,64]{1,0:T(1,128)S(1)} %copy-done.5, s32[1,32]{1,0:T(1,128)S(1)} %bitcast.1, bf16[1,64,128,128]{3,2,1,0:T(8,128)(2,1)S(1)} %copy-done, bf16[1,64,128,128]{3,2,1,0:T(8,128)(2,1)S(1)} %copy-done.1), custom_call_target="tpu_custom_call" | custom-call | tf_op jit(solution)/shard_map/prepare/pallas_call | solution.py:60
  4.2 0.0 collective-permute-done.block
  4.2 2.7 %collective-permute-start.2 = (bf16[1,32,1024]{2,1,0:T(8,128)(2,1)S(1)}, bf16[1,32,1024]{2,1,0:T(8,128)(2,1)S(1)}, u32[]{:S(2)}, u32[]{:S(2)}) collective-permute-start(bf16[1,32,1024]{2,1,0:T(8,128)(2,1)S(1)} %collective-permute-done.block), channel_id=1, source_target_pairs={{0,1},{1,0},{2,3},{3,2},{4,5},{5,4},{6,7},{7,6},{8,9},{9,8},{10,11... | collective-permute-start | bytes 196616 | tf_op jit(solution)/shard_map/ppermute | solution.py:258
  6.9 0.0 copy-done.2
  6.9 0.0 copy-done.3
  6.9 0.6 %first.1.others_0_ = f32[8,32,128]{2,1,0:T(8,128)S(1)} custom-call(s32[9,36]{1,0:T(8,128)S(1)} %get-tuple-element.11.lists, s32[32,128]{1,0:T(8,128)S(1)} %get-tuple-element.12.source, bf16[1,32,1024]{2,1,0:T(8,128)(2,1)S(1)} %collective-permute-done.block, bf16[64,128,128]{2,1,0:T(8,128)(2,1)S(1)} %get-tuple-element.13.weights, ...), custom_call_target="tpu_custom_call" | custom-call | flops 3000000000 | tf_op jit(solution)/shard_map/first/pallas_call | solution.py:60
  7.5 0.3 %collective-permute-done.2.block = bf16[1,32,1024]{2,1,0:T(8,128)(2,1)S(1)} collective-permute-done((bf16[1,32,1024]{2,1,0:T(8,128)(2,1)S(1)}, bf16[1,32,1024]{2,1,0:T(8,128)(2,1)S(1)}, u32[]{:S(2)}, u32[]{:S(2)}) %collective-permute-start.2) | collective-permute-done | bytes 65568 | tf_op jit(solution)/shard_map/ppermute | solution.py:258
  7.8 0.4 %second.1.others_0_ = f32[8,32,128]{2,1,0:T(8,128)S(1)} custom-call(s32[9,36]{1,0:T(8,128)S(1)} %get-tuple-element.11.lists, s32[32,128]{1,0:T(8,128)S(1)} %get-tuple-element.12.source, bf16[1,32,1024]{2,1,0:T(8,128)(2,1)S(1)} %collective-permute-done.2.block, bf16[64,128,128]{2,1,0:T(8,128)(2,1)S(1)} %get-tuple-element.13.weights, ...), custom_call_target="tpu_custom_call" | custom-call | tf_op jit(solution)/shard_map/second/pallas_call | solution.py:60
  8.2 0.0 collective-permute-done.1.block
  8.2 1.1 %far.1 = bf16[1,32,1024]{2,1,0:T(8,128)(2,1)} custom-call(s32[9,36]{1,0:T(8,128)S(1)} %get-tuple-element.11.lists, s32[32,128]{1,0:T(8,128)S(1)} %get-tuple-element.12.source, bf16[1,32,1024]{2,1,0:T(8,128)(2,1)S(1)} %collective-permute-done.1.block, bf16[64,128,128]{2,1,0:T(8,128)(2,1)S(1)} %get-tuple-element.13.weights, ...), custom_call_target="tpu_custom_call" | custom-call | tf_op jit(solution)/shard_map/far/pallas_call | solution.py:60
  (1 shorter events, 0.0 us)
Async XLA Ops:
  0.9 1.6 %copy-start = (bf16[1,64,128,128]{3,2,1,0:T(8,128)(2,1)S(1)}, bf16[1,64,128,128]{3,2,1,0:T(8,128)(2,1)}, u32[]{:S(2)}) copy-start(bf16[1,64,128,128]{3,2,1,0:T(8,128)(2,1)} %down_tiles.1) | copy-start | bytes 6291460
  0.9 2.2 %copy-start.1 = (bf16[1,64,128,128]{3,2,1,0:T(8,128)(2,1)S(1)}, bf16[1,64,128,128]{3,2,1,0:T(8,128)(2,1)}, u32[]{:S(2)}) copy-start(bf16[1,64,128,128]{3,2,1,0:T(8,128)(2,1)} %up_tiles.1) | copy-start | bytes 6291460
  0.9 2.2 %copy-start.4 = (s32[1,64]{1,0:T(1,128)S(1)}, s32[1,64]{1,0:T(1,128)}, u32[]{:S(2)}) copy-start(s32[1,64]{1,0:T(1,128)} %tile_rows.1) | copy-start | bytes 772
  0.9 2.2 %copy-start.5 = (s32[1,64]{1,0:T(1,128)S(1)}, s32[1,64]{1,0:T(1,128)}, u32[]{:S(2)}) copy-start(s32[1,64]{1,0:T(1,128)} %tile_cols.1) | copy-start | bytes 772
  0.9 2.2 %copy-start.6 = (s32[32]{0:T(128)S(1)}, s32[32]{0:T(128)}, u32[]{:S(2)}) copy-start(s32[32]{0:T(128)} %param.13) | copy-start | bytes 388
  0.9 3.3 %collective-permute-start = (bf16[1,32,1024]{2,1,0:T(8,128)(2,1)S(1)}, bf16[1,32,1024]{2,1,0:T(8,128)(2,1)S(1)}, u32[]{:S(2)}, u32[]{:S(2)}) collective-permute-start(bf16[1,32,1024]{2,1,0:T(8,128)(2,1)S(1)} %broadcast_select_fusion.block), channel_id=1, source_target_pairs={{0,17},{1,16},{2,18},{3,19},{4,20},{5,21},{6,22},{7,23},{8,24},{9,... | collective-permute-start | bytes 196616 | tf_op jit(solution)/shard_map/ppermute | solution.py:45
  1.2 7.0 %collective-permute-start.1 = (bf16[1,32,1024]{2,1,0:T(8,128)(2,1)S(1)}, bf16[1,32,1024]{2,1,0:T(8,128)(2,1)S(1)}, u32[]{:S(2)}, u32[]{:S(2)}) collective-permute-start(bf16[1,32,1024]{2,1,0:T(8,128)(2,1)S(1)} %duplicate.1), channel_id=1, source_target_pairs={{0,16},{1,18},{2,17},{3,20},{4,19},{5,22},{6,21},{7,24},{8,23},{9,... | collective-permute-start | bytes 196616 | tf_op jit(solution)/shard_map/ppermute | solution.py:45
  3.1 3.8 %copy-start.2 = (bf16[1,32,1024]{2,1,0:T(8,128)(2,1)S(1)}, bf16[1,32,1024]{2,1,0:T(8,128)(2,1)}, u32[]{:S(2)}) copy-start(bf16[1,32,1024]{2,1,0:T(8,128)(2,1)} %up.5) | copy-start | bytes 196612
  3.1 3.8 %copy-start.3 = (bf16[1,32,1024]{2,1,0:T(8,128)(2,1)S(1)}, bf16[1,32,1024]{2,1,0:T(8,128)(2,1)}, u32[]{:S(2)}) copy-start(bf16[1,32,1024]{2,1,0:T(8,128)(2,1)} %down.5) | copy-start | bytes 196612
  4.2 3.6 %collective-permute-start.2 = (bf16[1,32,1024]{2,1,0:T(8,128)(2,1)S(1)}, bf16[1,32,1024]{2,1,0:T(8,128)(2,1)S(1)}, u32[]{:S(2)}, u32[]{:S(2)}) collective-permute-start(bf16[1,32,1024]{2,1,0:T(8,128)(2,1)S(1)} %collective-permute-done.block), channel_id=1, source_target_pairs={{0,1},{1,0},{2,3},{3,2},{4,5},{5,4},{6,7},{7,6},{8,9},{9,8},{10,11... | collective-permute-start | bytes 196616 | tf_op jit(solution)/shard_map/ppermute | solution.py:258
